TPU v7x, 128 devices: a whole 4x4x4 slice. The times are simulated.
128 devices in a mesh: dp: 8 (over x, y_lo), fsdp: 16 (over y_hi, z, core).
Axes of the slice: x: 4, y: 4 (y_hi: 2, y_lo: 2; y = y_hi * 2 + y_lo), z: 4, core: 2. Of those that a mesh axis runs over, the one named last changes fastest.
Arguments:
- tokens: bfloat16 [16384, 2048], P(('dp', 'fsdp')), may hold values from -6 to 6
- cotangent: bfloat16 [16384, 2048], P(('dp', 'fsdp')), may hold values from -6 to 6
- seq_rows: int32 [8, 2], P('dp'), may hold values from 0 to 128, as said below
- qkv_weight: bfloat16 [2048, 4096], P(('dp', 'fsdp')), may hold values from -0.125 to 0.125
- out_weight: bfloat16 [2048, 2048], P(('dp', 'fsdp')), may hold values from -1 to 1
- attn_gain: bfloat16 [2048], P(('dp', 'fsdp')), may hold values from 0.5 to 1.5
- query_gain: bfloat16 [128], P(('dp', 'fsdp')), may hold values from 0.25 to 1.75
- key_gain: bfloat16 [128], P(('dp', 'fsdp')), may hold values from 0.25 to 1.75
- gate_up_weight: bfloat16 [2048, 12288], P(('dp', 'fsdp')), may hold values from -0.125 to 0.125
- down_weight: bfloat16 [2048, 6144], P(('dp', 'fsdp')), may hold values from -0.078125 to 0.078125
- mlp_gain: bfloat16 [2048], P(('dp', 'fsdp')), may hold values from 0.5 to 1.5
Outputs:
- block_out: bfloat16 [16384, 2048], P(('dp', 'fsdp'))
- tokens_grad: float32 [16384, 2048], P(('dp', 'fsdp'))
- qkv_grad: float32 [2048, 4096], P(('dp', 'fsdp'))
- out_grad: float32 [2048, 2048], P(('dp', 'fsdp'))
- attn_gain_grad: float32 [2048], P(('dp', 'fsdp'))
- query_gain_grad: float32 [128], P(('dp', 'fsdp'))
- key_gain_grad: float32 [128], P(('dp', 'fsdp'))
- gate_up_grad: float32 [2048, 12288], P(('dp', 'fsdp'))
- down_grad: float32 [2048, 6144], P(('dp', 'fsdp'))
- mlp_gain_grad: float32 [2048], P(('dp', 'fsdp'))
Inputs may be any that keep to these rules, and one draw needn't show every extreme that they name: Row g of seq_rows lists, for each sequence of dp index g in order, how many rows of it each device of that index holds; nonzero entries come first and are 64 or more; a row sums to 64 or more and to 128 at most; in some row the first entry is 128.
All inputs are finite; a program needn't handle non-finite values.
Results may differ from a plain program's by a relative error of at most 0.03.
Values may be sent and summed in bfloat16 or wider, within the bound.
A program may use at most 512 MiB of HBM per device.

v0:
```python
import math

import jax
import jax.numpy as jnp
from jax import lax
from jax.sharding import PartitionSpec as P

QUERY_HEADS = 16
KEY_VALUE_HEADS = 8
HEAD_SIZE = 128
FF = 6144
QUERY_FEATURES = 2048
KEY_FEATURES = 1024


rope_base = 1000000.0


def rms_scale(values, gain):
    return values * lax.rsqrt(jnp.mean(values * values, axis=-1, keepdims=True) + 1e-06) * gain


def row_layout(seq_counts, device, token_rows):
    seq_ends = jnp.cumsum(seq_counts)
    starts = seq_ends - seq_counts
    row_place = jnp.arange(token_rows, dtype=jnp.int32)
    inside = (
        (row_place[:, None] >= starts[None, :]) & (row_place[:, None] < seq_ends[None, :])
    ).astype(jnp.int32)
    slot_ids = jnp.arange(seq_counts.shape[0], dtype=jnp.int32)
    in_sequence = row_place < seq_ends[-1]
    segment = jnp.where(in_sequence, jnp.sum(inside * slot_ids[None, :], axis=1), -1)
    length = jnp.sum(inside * seq_counts[None, :], axis=1)
    seq_begin = jnp.sum(inside * starts[None, :], axis=1)
    position = device * length[None, :] + row_place[None, :] - seq_begin[None, :]
    return (position, segment)


def rope_tables(position):
    half_dim = HEAD_SIZE // 2
    frequency = jnp.exp(
        jnp.arange(half_dim, dtype=jnp.float32) * (-2.0 * math.log(rope_base) / HEAD_SIZE)
    )
    angles = position.astype(jnp.float32)[:, None] * frequency[None, :]
    return (jnp.cos(angles)[:, None, :], jnp.sin(angles)[:, None, :])


def rotate(values, cosine, sine_part):
    half_dim = HEAD_SIZE // 2
    first_half = values[..., :half_dim]
    second_half = values[..., half_dim:]
    return jnp.concatenate(
        [
            first_half * cosine - second_half * sine_part,
            second_half * cosine + first_half * sine_part,
        ],
        axis=-1,
    )


def prepare(projected_rows, query_scale, key_scale, cosine, sine_part):
    token_rows = projected_rows.shape[0]
    query_rows = projected_rows[:, :QUERY_FEATURES].reshape(token_rows, QUERY_HEADS, HEAD_SIZE)
    unrotated_keys = projected_rows[:, QUERY_FEATURES : QUERY_FEATURES + KEY_FEATURES].reshape(
        token_rows, KEY_VALUE_HEADS, HEAD_SIZE
    )
    unrotated_values = projected_rows[:, QUERY_FEATURES + KEY_FEATURES :].reshape(
        token_rows, KEY_VALUE_HEADS, HEAD_SIZE
    )
    query_rows = rotate(rms_scale(query_rows, query_scale), cosine, sine_part)
    unrotated_keys = rotate(rms_scale(unrotated_keys, key_scale), cosine, sine_part)
    return (query_rows, unrotated_keys, unrotated_values)


def swiglu(joined):
    return jax.nn.silu(joined[:, :FF]) * joined[:, FF:]


def contract_last(left_arr, right_arr):
    return lax.dot_general(
        left_arr, right_arr, (((1,), (1,)), ((), ())), preferred_element_type=jnp.float32
    )


def contract_first(left_arr, right_arr):
    return lax.dot_general(
        left_arr, right_arr, (((0,), (0,)), ((), ())), preferred_element_type=jnp.float32
    )


def block_probs(query_part, key_part, visible, score_scale):
    raw_scores = jnp.einsum(
        "tkrd,skd->krts", query_part, key_part, preferred_element_type=jnp.float32
    )
    return jnp.where(visible[None, None], raw_scores * score_scale, -1e30)


def local(
    tokens,
    cotangent,
    seq_rows,
    qkv_weight,
    out_weight,
    attn_gain,
    query_gain,
    key_gain,
    gate_up_weight,
    down_weight,
    mlp_gain,
):
    token_rows = tokens.shape[0]
    fsdp_size = lax.axis_size("fsdp")
    own_index = lax.axis_index("fsdp")
    grouped_rows = token_rows * fsdp_size
    seq_counts = seq_rows[0]
    position_all, segment = row_layout(
        seq_counts, jnp.arange(fsdp_size, dtype=jnp.int32)[:, None], token_rows
    )
    own_position = lax.dynamic_index_in_dim(position_all, own_index, 0, keepdims=False)
    key_position = position_all.reshape(grouped_rows)
    key_segment = jnp.tile(segment, fsdp_size)
    query_index = own_index * token_rows + jnp.arange(token_rows, dtype=jnp.int32)
    key_index = jnp.arange(grouped_rows, dtype=jnp.int32)
    visible = (segment[:, None] == key_segment[None, :]) & (segment[:, None] >= 0) & (
        key_position[None, :] <= own_position[:, None]
    ) | (query_index[:, None] == key_index[None, :])
    score_scale = HEAD_SIZE ** (-0.5)
    repeat_factor = QUERY_HEADS // KEY_VALUE_HEADS
    block_list = KEY_VALUE_HEADS // 2
    cosine, sine_part = rope_tables(own_position)
    attn_full = (
        lax.all_gather(qkv_weight, ("dp", "fsdp"), axis=0, tiled=True),
        lax.all_gather(out_weight, ("dp", "fsdp"), axis=0, tiled=True),
        lax.all_gather(attn_gain, ("dp", "fsdp"), axis=0, tiled=True),
        lax.all_gather(query_gain, ("dp", "fsdp"), axis=0, tiled=True),
        lax.all_gather(key_gain, ("dp", "fsdp"), axis=0, tiled=True),
    )
    inputs_f = tokens.astype(jnp.float32)
    gain_a = attn_full[2].astype(jnp.float32)
    gain_q = attn_full[3].astype(jnp.float32)
    gain_k = attn_full[4].astype(jnp.float32)
    normed = rms_scale(inputs_f, gain_a).astype(jnp.bfloat16)
    projected_rows = jnp.dot(normed, attn_full[0], preferred_element_type=jnp.float32)
    query_rows, keys_rot, unrotated_values = prepare(
        projected_rows, gain_q, gain_k, cosine, sine_part
    )
    query_head_rows = query_rows.astype(jnp.bfloat16).reshape(
        token_rows, KEY_VALUE_HEADS, repeat_factor, HEAD_SIZE
    )
    key_local = keys_rot.astype(jnp.bfloat16).reshape(token_rows, KEY_FEATURES)
    value_local = unrotated_values.astype(jnp.bfloat16).reshape(token_rows, KEY_FEATURES)
    grouped_keys, grouped_values = (
        lax.all_gather(key_local, "fsdp", axis=0, tiled=True),
        lax.all_gather(value_local, "fsdp", axis=0, tiled=True),
    )
    key_head_rows = grouped_keys.reshape(grouped_rows, KEY_VALUE_HEADS, HEAD_SIZE)
    value_head_rows = grouped_values.reshape(grouped_rows, KEY_VALUE_HEADS, HEAD_SIZE)
    output_list = []
    totals_list = []
    for block in range(block_list):
        query_part = query_head_rows[:, 2 * block : 2 * block + 2]
        key_part = key_head_rows[:, 2 * block : 2 * block + 2]
        value_part = value_head_rows[:, 2 * block : 2 * block + 2]
        scores = block_probs(query_part, key_part, visible, score_scale)
        peak_val = jnp.max(scores, axis=-1, keepdims=True)
        totals = peak_val + jnp.log(jnp.sum(jnp.exp(scores - peak_val), axis=-1, keepdims=True))
        probs = jnp.exp(scores - totals).astype(jnp.bfloat16)
        output_list.append(
            jnp.einsum("krts,skd->tkrd", probs, value_part, preferred_element_type=jnp.float32)
        )
        totals_list.append(totals)
    attended = (
        jnp.concatenate(output_list, axis=1)
        .reshape(token_rows, QUERY_FEATURES)
        .astype(jnp.bfloat16)
    )
    branch = contract_last(attended, attn_full[1])
    middle = inputs_f + branch
    mlp_full = (
        lax.all_gather(gate_up_weight, ("dp", "fsdp"), axis=0, tiled=True),
        lax.all_gather(down_weight, ("dp", "fsdp"), axis=0, tiled=True),
        lax.all_gather(mlp_gain, ("dp", "fsdp"), axis=0, tiled=True),
    )
    gain_m = mlp_full[2].astype(jnp.float32)
    normed_m = rms_scale(middle, gain_m).astype(jnp.bfloat16)
    joined = jnp.dot(normed_m, mlp_full[0], preferred_element_type=jnp.float32)
    hidden = swiglu(joined).astype(jnp.bfloat16)
    mlp_out = contract_last(hidden, mlp_full[1])
    block_out = (middle + mlp_out).astype(jnp.bfloat16)
    mlp_back = (
        lax.all_gather(gate_up_weight, ("dp", "fsdp"), axis=0, tiled=True),
        lax.all_gather(down_weight, ("dp", "fsdp"), axis=0, tiled=True),
        lax.all_gather(mlp_gain, ("dp", "fsdp"), axis=0, tiled=True),
    )
    back_gain_m = mlp_back[2].astype(jnp.float32)
    hidden_grad = jnp.dot(cotangent, mlp_back[1], preferred_element_type=jnp.float32)
    _, swiglu_back = jax.vjp(swiglu, joined)
    joined_grad = swiglu_back(hidden_grad)[0].astype(jnp.bfloat16)
    normed_m_grad = contract_last(joined_grad, mlp_back[0])
    _, norm_m_back = jax.vjp(rms_scale, middle, back_gain_m)
    middle_part, gain_m_grad = norm_m_back(normed_m_grad)
    middle_grad = cotangent.astype(jnp.float32) + middle_part
    down_term = contract_first(cotangent, hidden)
    down_grad, mlp_gain_grad = (
        lax.psum_scatter(down_term, ("dp", "fsdp"), scatter_dimension=0, tiled=True),
        lax.psum_scatter(gain_m_grad, ("dp", "fsdp"), scatter_dimension=0, tiled=True),
    )
    gate_up_grad = lax.psum_scatter(
        contract_first(normed_m, joined_grad), ("dp", "fsdp"), scatter_dimension=0, tiled=True
    )
    attn_back = (
        lax.all_gather(qkv_weight, ("dp", "fsdp"), axis=0, tiled=True),
        lax.all_gather(out_weight, ("dp", "fsdp"), axis=0, tiled=True),
        lax.all_gather(attn_gain, ("dp", "fsdp"), axis=0, tiled=True),
        lax.all_gather(query_gain, ("dp", "fsdp"), axis=0, tiled=True),
        lax.all_gather(key_gain, ("dp", "fsdp"), axis=0, tiled=True),
    )
    back_gain_a = attn_back[2].astype(jnp.float32)
    back_gain_q = attn_back[3].astype(jnp.float32)
    back_gain_k = attn_back[4].astype(jnp.float32)
    branch_grad = middle_grad.astype(jnp.bfloat16)
    attended_gradient = jnp.dot(branch_grad, attn_back[1], preferred_element_type=jnp.float32)
    head_gradients = attended_gradient.astype(jnp.bfloat16).reshape(
        token_rows, KEY_VALUE_HEADS, repeat_factor, HEAD_SIZE
    )
    out_term = contract_first(branch_grad, attended)
    query_grad_list = []
    key_grad_list = []
    value_grad_list = []
    for block in range(block_list):
        query_part = query_head_rows[:, 2 * block : 2 * block + 2]
        key_part = key_head_rows[:, 2 * block : 2 * block + 2]
        value_part = value_head_rows[:, 2 * block : 2 * block + 2]
        grad_part = head_gradients[:, 2 * block : 2 * block + 2]
        scores = block_probs(query_part, key_part, visible, score_scale)
        probs_full = jnp.exp(scores - totals_list[block])
        probs_low = probs_full.astype(jnp.bfloat16)
        probs_grad = jnp.einsum(
            "tkrd,skd->krts", grad_part, value_part, preferred_element_type=jnp.float32
        )
        inner_sum = jnp.sum(probs_full * probs_grad, axis=-1, keepdims=True)
        raw_grad = (probs_full * (probs_grad - inner_sum) * score_scale).astype(jnp.bfloat16)
        query_grad_list.append(
            jnp.einsum("krts,skd->tkrd", raw_grad, key_part, preferred_element_type=jnp.float32)
        )
        key_grad_list.append(
            jnp.einsum("krts,tkrd->skd", raw_grad, query_part, preferred_element_type=jnp.float32)
        )
        value_grad_list.append(
            jnp.einsum("krts,tkrd->skd", probs_low, grad_part, preferred_element_type=jnp.float32)
        )
    query_gradient = jnp.concatenate(query_grad_list, axis=1).reshape(
        token_rows, QUERY_HEADS, HEAD_SIZE
    )
    key_terms = jnp.concatenate(key_grad_list, axis=1).reshape(grouped_rows, KEY_FEATURES)
    value_terms = jnp.concatenate(value_grad_list, axis=1).reshape(grouped_rows, KEY_FEATURES)
    key_gradient, value_gradient = (
        lax.psum_scatter(
            key_terms.astype(jnp.bfloat16), "fsdp", scatter_dimension=0, tiled=True
        ).astype(jnp.float32),
        lax.psum_scatter(
            value_terms.astype(jnp.bfloat16), "fsdp", scatter_dimension=0, tiled=True
        ).astype(jnp.float32),
    )

    def prepare_local(projection, query_scale, key_scale):
        return prepare(projection, query_scale, key_scale, cosine, sine_part)

    _, prepare_back = jax.vjp(prepare_local, projected_rows, back_gain_q, back_gain_k)
    projected_grad, gain_q_grad, gain_k_grad = prepare_back(
        (
            query_gradient,
            key_gradient.reshape(token_rows, KEY_VALUE_HEADS, HEAD_SIZE),
            value_gradient.reshape(token_rows, KEY_VALUE_HEADS, HEAD_SIZE),
        )
    )
    projected_low = projected_grad.astype(jnp.bfloat16)
    normed_grad = contract_last(projected_low, attn_back[0])
    _, norm_a_back = jax.vjp(rms_scale, inputs_f, back_gain_a)
    input_part, gain_a_grad = norm_a_back(normed_grad)
    tokens_grad = middle_grad + input_part
    qkv_grad = lax.psum_scatter(
        contract_first(normed, projected_low), ("dp", "fsdp"), scatter_dimension=0, tiled=True
    )
    out_grad, attn_gain_grad, query_gain_grad, key_gain_grad = (
        lax.psum_scatter(out_term, ("dp", "fsdp"), scatter_dimension=0, tiled=True),
        lax.psum_scatter(gain_a_grad, ("dp", "fsdp"), scatter_dimension=0, tiled=True),
        lax.psum_scatter(gain_q_grad, ("dp", "fsdp"), scatter_dimension=0, tiled=True),
        lax.psum_scatter(gain_k_grad, ("dp", "fsdp"), scatter_dimension=0, tiled=True),
    )
    return (
        block_out,
        tokens_grad,
        qkv_grad,
        out_grad,
        attn_gain_grad,
        query_gain_grad,
        key_gain_grad,
        gate_up_grad,
        down_grad,
        mlp_gain_grad,
    )


def solution(mesh):
    placed = (
        P(("dp", "fsdp"), None),
        P(("dp", "fsdp"), None),
        P("dp", None),
        P(("dp", "fsdp"), None),
        P(("dp", "fsdp"), None),
        P(("dp", "fsdp")),
        P(("dp", "fsdp")),
        P(("dp", "fsdp")),
        P(("dp", "fsdp"), None),
        P(("dp", "fsdp"), None),
        P(("dp", "fsdp")),
    )
    return jax.shard_map(
        local,
        mesh=mesh,
        in_specs=placed,
        out_specs=(
            P(("dp", "fsdp"), None),
            P(("dp", "fsdp"), None),
            P(("dp", "fsdp"), None),
            P(("dp", "fsdp"), None),
            P(("dp", "fsdp")),
            P(("dp", "fsdp")),
            P(("dp", "fsdp")),
            P(("dp", "fsdp"), None),
            P(("dp", "fsdp"), None),
            P(("dp", "fsdp")),
        ),
        check_vma=False,
    )
```

profile of v0, /device:TPU:1, one launch (start us, length us, event | category | flops | bytes accessed | tf_op | source)
XLA Modules:
  0.0 4207.4 jit_solution(7924663853230848505)
XLA Ops:
  11.2 69.0 %all-reduce.18 = (bf16[2048]{0:T(1024)(128)(2,1)S(1)}, bf16[128]{0:T(256)(128)(2,1)S(1)}, bf16[128]{0:T(256)(128)(2,1)S(1)}, bf16[2048]{0:T(1024)(128)(2,1)S(1)}) all-reduce(bf16[2048]{0:T(1024)(128)(2,1)S(1)} %dynamic-update-slice, bf16[128]{0:T(256)(128)(2,1)S(1)} %dynamic-update-slice.1, ...), channel_id=1, replica_groups=mesh['dp'=8,'fsdp'=16] {'dp','fsdp'}, use_global_device_ids=true, to_apply=%add.9 | all-reduce | flops 4352 | bytes 17408
  80.2 1.2 fusion.94
  81.5 144.9 %all-gather.7.cloned.1.call-done = bf16[2048,4096]{1,0:T(8,128)(2,1)} async-done(((bf16[16,4096]{1,0:T(8,128)(2,1)}), bf16[2048,4096]{1,0:T(8,128)(2,1)}) %all-gather.7.cloned.1.call-update) | async-done | bytes 16777232 | tf_op jit(solution)/shard_map/all_gather | solution.py:132
  226.4 8.4 fusion.117
  241.5 1.4 fusion.96
  246.0 44.7 %all-gather.9.cloned.1.call-done = bf16[2048,1024]{1,0:T(8,128)(2,1)} async-done(((bf16[128,1024]{1,0:T(8,128)(2,1)}), bf16[2048,1024]{1,0:T(8,128)(2,1)}) %all-gather.9.cloned.1.call-update) | async-done | bytes 4194320 | tf_op jit(solution)/shard_map/all_gather | solution.py:154
  290.6 6.7 copy.420
  297.3 50.7 %all-gather.11.cloned.1.call-done = bf16[2048,1024]{0,1:T(8,128)(2,1)} async-done(((bf16[128,1024]{0,1:T(8,128)(2,1)}), bf16[2048,1024]{0,1:T(8,128)(2,1)}) %all-gather.11.cloned.1.call-update) | async-done | bytes 4194320 | tf_op jit(solution)/shard_map/all_gather | solution.py:153
  348.1 2.3 fusion.171
  355.6 2.8 copy-done.8
  361.9 187.8 %all-gather.13.cloned.1.call-done = bf16[2048,2048]{1,0:T(8,128)(2,1)} async-done(((bf16[16,2048]{1,0:T(8,128)(2,1)}), bf16[2048,2048]{1,0:T(8,128)(2,1)}) %all-gather.13.cloned.1.call-update) | async-done | bytes 8388624 | tf_op jit(solution)/shard_map/all_gather | solution.py:133
  549.7 6.4 multiply_reduce_fusion.4
  556.1 273.6 %all-gather.15.cloned.1.call-done = bf16[2048,12288]{1,0:T(8,128)(2,1)} async-done(((bf16[16,12288]{1,0:T(8,128)(2,1)}), bf16[2048,12288]{1,0:T(8,128)(2,1)}) %all-gather.15.cloned.1.call-update) | async-done | bytes 50331664 | tf_op jit(solution)/shard_map/all_gather | solution.py:180
  829.7 20.8 fusion.164
  850.6 209.0 %all-gather.17.cloned.1.call-done = bf16[2048,6144]{1,0:T(8,128)(2,1)} async-done(((bf16[16,6144]{1,0:T(8,128)(2,1)}), bf16[2048,6144]{1,0:T(8,128)(2,1)}) %all-gather.17.cloned.1.call-update) | async-done | bytes 25165840 | tf_op jit(solution)/shard_map/all_gather | solution.py:181
  1059.5 16.0 fusion.111
  1075.6 25.2 multiply_reduce_fusion
  1100.8 1.7 fusion.92
  1102.5 5.0 convolution_convert_fusion
  1107.8 4.1 fusion.100
  1111.9 2.7 fusion.99
  1114.6 2.7 fusion.98
  1117.2 2.7 fusion.97
  1120.0 8.9 fusion.47
  1128.9 9.0 fusion.48
  1137.9 8.8 fusion.50
  1146.7 9.2 fusion.49
  1155.9 3.8 pad_maximum_fusion.1
  1159.7 6.4 copy.416
  1166.2 3.1 fusion.51
  1169.3 3.1 fusion.52
  1173.9 2.3 pad_maximum_fusion
  1176.2 6.5 copy.414
  1183.8 8.2 fusion.112
  1192.5 8.0 fusion.82
  1200.4 8.2 fusion.83
  1208.6 8.0 fusion.85
  1216.7 8.2 fusion.84
  1225.0 1.4 copy.428
  1226.4 1.4 copy.429
  1227.8 1.8 multiply_add_fusion.1
  1229.6 1.4 multiply_reduce_fusion.1
  1231.3 2.1 add_add_fusion.1
  1233.3 1.6 copy.348
  1235.0 9.2 reduce-scatter.21.cloned.1.call-done
  1244.2 1.1 copy.417
  1247.4 1.4 multiply_add_fusion.3
  1250.0 1.3 add_add_fusion.3
  1251.3 1.2 copy.335
  1252.6 75.6 %reduce-scatter.19.cloned.1.call-done = bf16[128,1024]{1,0:T(8,128)(2,1)} async-done(((bf16[2048,1024]{1,0:T(8,128)(2,1)}), bf16[128,1024]{1,0:T(8,128)(2,1)}) %reduce-scatter.19.cloned.1.call-update) | async-done | bytes 262160
  1329.3 13.6 fusion.115
  1343.0 1.3 copy-done.16
  1344.5 19.5 convolution_bitcast_fusion
  1364.1 48.9 %copy.418 = f32[2048,6144]{1,0:T(8,128)} copy(f32[2048,6144]{0,1:T(8,128)} %convolution_bitcast_fusion) | data formatting | bytes 100663296
  1413.0 1.2 copy-done.7
  1414.2 35.9 fusion.109
  1450.1 14.0 fusion.55
  1464.2 12.2 fusion.91
  1476.5 67.3 %all-reduce.17 = (f32[2048]{0:T(1024)S(1)}, f32[128]{0:T(128)S(1)}, f32[128]{0:T(128)S(1)}, f32[2048]{0:T(1024)S(1)}) all-reduce(f32[2048]{0:T(1024)S(1)} %get-tuple-element.74, f32[128]{0:T(128)S(1)} %copy-done.30, f32[128]{0:T(128)S(1)} %copy-done.31, f32[2048]{0:T(1024)S(1)} %copy-done.29), channel_id=6, replica_groups=mesh['dp'=8,'fsdp'=16] {'dp','fsdp'}, use_global_device_ids=true, to_apply=%region_29.30.clone | all-reduce | flops 4352 | bytes 34816
  1546.1 1.3 fusion.93
  1547.4 442.4 %reduce-scatter.15.cloned.1.call-done = f32[16,2048]{1,0:T(8,128)} async-done(((f32[2048,2048]{1,0:T(8,128)}), f32[16,2048]{1,0:T(8,128)}) %reduce-scatter.15.cloned.1.call-update) | async-done | bytes 131088 | tf_op jit(solution)/shard_map/reduce_scatter | solution.py:286
  1989.7 689.6 %reduce-scatter.13.cloned.1.call-done = f32[16,4096]{1,0:T(8,128)} async-done(((f32[2048,4096]{1,0:T(8,128)}), f32[16,4096]{1,0:T(8,128)}) %reduce-scatter.13.cloned.1.call-update) | async-done | bytes 262160 | tf_op jit(solution)/shard_map/reduce_scatter | solution.py:282
  2679.3 718.4 %reduce-scatter.23.cloned.1.call-done = f32[16,6144]{1,0:T(8,128)} async-done(((f32[2048,6144]{1,0:T(8,128)}), f32[16,6144]{1,0:T(8,128)}) %reduce-scatter.23.cloned.1.call-update) | async-done | bytes 393232
  3397.8 802.5 %reduce-scatter.17.cloned.1.call-done = f32[16,12288]{1,0:T(8,128)} async-done(((f32[2048,12288]{1,0:T(8,128)}), f32[16,12288]{1,0:T(8,128)}) %reduce-scatter.17.cloned.1.call-update) | async-done | bytes 786448 | tf_op jit(solution)/shard_map/reduce_scatter | solution.py:208
  (176 shorter events, 31.5 us)
Async XLA Ops:
  7.2 219.2 %all-gather.7.cloned.1.call-start = ((), (), s32[]{:S(2)}) async-start(), calls=%async_computation.6 | async-start | bytes 16908288 | tf_op jit(solution)/shard_map/all_gather | solution.py:132
  7.9 282.7 %all-gather.9.cloned.1.call-start = ((), (), s32[]{:S(2)}) async-start(), calls=%async_computation.7 | async-start | bytes 4456448 | tf_op jit(solution)/shard_map/all_gather | solution.py:154
  81.4 153.4 %copy-start.32 = (f32[128]{0:T(128)}, f32[128]{0:T(128)S(1)}, u32[]{:S(2)}) copy-start(f32[128]{0:T(128)S(1)} %fusion.94) | copy-start | bytes 1540
  81.4 154.2 %copy-start.34 = (s32[1,2]{1,0:T(1,128)S(1)}, s32[1,2]{1,0:T(1,128)}, u32[]{:S(2)}) copy-start(s32[1,2]{1,0:T(1,128)} %param.13) | copy-start | bytes 28
  235.6 112.5 %all-gather.11.cloned.1.call-start = ((), (), s32[]{:S(2)}) async-start(), calls=%async_computation.8 | async-start | bytes 4456448 | tf_op jit(solution)/shard_map/all_gather | solution.py:153
  236.4 5.1 copy-start.14
  238.4 311.3 %all-gather.13.cloned.1.call-start = ((), (), s32[]{:S(2)}) async-start(), calls=%async_computation.9 | async-start | bytes 8454144 | tf_op jit(solution)/shard_map/all_gather | solution.py:133
  239.0 590.7 %all-gather.15.cloned.1.call-start = ((), (), s32[]{:S(2)}) async-start(), calls=%async_computation.10 | async-start | bytes 50724864 | tf_op jit(solution)/shard_map/all_gather | solution.py:180
  239.6 819.9 %all-gather.17.cloned.1.call-start = ((), (), s32[]{:S(2)}) async-start(), calls=%async_computation.11 | async-start | bytes 25362432 | tf_op jit(solution)/shard_map/all_gather | solution.py:181
  240.2 1004.0 %reduce-scatter.21.cloned.1.call-start = ((), (), s32[]{:S(2)}) async-start(), calls=%async_computation.16 | async-start | bytes 4456448
  240.8 859.9 %copy-start.24 = (f32[2048]{0:T(1024)}, f32[2048]{0:T(1024)S(1)}, u32[]{:S(2)}) copy-start(f32[2048]{0:T(1024)S(1)} %convert_element_type.117) | copy-start | bytes 24580
  348.1 2.9 copy-start.21
  350.4 5.2 copy-start
  351.9 7.3 copy-start.2
  353.4 6.7 copy-start.4
  354.0 4.3 copy-start.8
  355.0 6.0 copy-start.5
  361.0 188.7 %copy-start.12 = (bf16[128,2048]{1,0:T(8,128)(2,1)S(1)}, bf16[128,2048]{1,0:T(8,128)(2,1)}, u32[]{:S(2)}) copy-start(bf16[128,2048]{1,0:T(8,128)(2,1)} %param.11) | copy-start | bytes 1572868
  361.9 194.2 %copy-start.19 = (bf16[128,8,2,128]{0,3,2,1:T(8,128)(2,1)}, bf16[128,8,2,128]{0,3,2,1:T(8,128)(2,1)S(1)}, u32[]{:S(2)}) copy-start(bf16[128,8,2,128]{0,3,2,1:T(8,128)(2,1)S(1)} %pad_maximum_fusion.3) | copy-start | bytes 1572868
  556.1 544.6 %copy-start.6 = (f32[128,2048]{1,0:T(8,128)}, f32[128,2048]{1,0:T(8,128)S(1)}, u32[]{:S(2)}) copy-start(f32[128,2048]{1,0:T(8,128)S(1)} %get-tuple-element.121) | copy-start | bytes 3145732
  556.1 544.6 %copy-start.27 = (f32[128]{0:T(128)}, f32[128]{0:T(128)S(1)}, u32[]{:S(2)}) copy-start(f32[128]{0:T(128)S(1)} %fusion.149) | copy-start | bytes 1540
  829.7 229.8 %copy-start.22 = (bf16[128,2048]{1,0:T(8,128)(2,1)S(1)}, bf16[128,2048]{1,0:T(8,128)(2,1)}, u32[]{:S(2)}) copy-start(bf16[128,2048]{1,0:T(8,128)(2,1)} %param.12) | copy-start | bytes 1572868
  1102.5 80.3 %copy-start.10 = (f32[128,2048]{1,0:T(8,128)}, f32[128,2048]{1,0:T(8,128)S(1)}, u32[]{:S(2)}) copy-start(f32[128,2048]{1,0:T(8,128)S(1)} %fusion.92) | copy-start | bytes 3145732
  1107.8 4.1 copy-start.9
  1114.6 5.4 copy-start.26
  1166.1 162.0 %reduce-scatter.19.cloned.1.call-start = ((), (), s32[]{:S(2)}) async-start(), calls=%async_computation.15 | async-start | bytes 4456448
  1166.2 6.2 copy-start.3
  1169.3 3.8 copy-start.1
  1182.7 1.1 copy-start.20
  1182.7 807.0 %reduce-scatter.15.cloned.1.call-start = ((), (), s32[]{:S(2)}) async-start(), calls=%async_computation.13 | async-start | bytes 16908288 | tf_op jit(solution)/shard_map/reduce_scatter | solution.py:286
  1192.0 1487.3 %reduce-scatter.13.cloned.1.call-start = ((), (), s32[]{:S(2)}) async-start(), calls=%async_computation.12 | async-start | bytes 33816576 | tf_op jit(solution)/shard_map/reduce_scatter | solution.py:282
  1233.3 15.5 copy-start.15
  1235.0 94.3 %copy-start.17 = (f32[128,16,128]{0,2,1:T(8,128)}, f32[128,16,128]{0,2,1:T(8,128)S(1)}, u32[]{:S(2)}) copy-start(f32[128,16,128]{0,2,1:T(8,128)S(1)} %copy.348) | copy-start | bytes 3145732
  1247.4 81.9 %copy-start.13 = (bf16[128,2048]{1,0:T(8,128)(2,1)S(1)}, bf16[128,2048]{1,0:T(8,128)(2,1)}, u32[]{:S(2)}) copy-start(bf16[128,2048]{1,0:T(8,128)(2,1)} %param.11) | copy-start | bytes 1572868
  1252.6 90.4 %copy-start.18 = (f32[128,8,128]{0,2,1:T(8,128)}, f32[128,8,128]{0,2,1:T(8,128)S(1)}, u32[]{:S(2)}) copy-start(f32[128,8,128]{0,2,1:T(8,128)S(1)} %copy.335) | copy-start | bytes 1572868
  1343.0 1.4 copy-start.16
  1343.0 1.5 copy-start.23
  1343.0 2054.8 %reduce-scatter.23.cloned.1.call-start = ((), (), s32[]{:S(2)}) async-start(), calls=%async_computation.17 | async-start | bytes 50724864
  1413.0 1.2 copy-start.7
  1413.0 1.2 copy-start.25
  1413.0 1.2 copy-start.28
  1413.0 2787.3 %reduce-scatter.17.cloned.1.call-start = ((), (), s32[]{:S(2)}) async-start(), calls=%async_computation.14 | async-start | bytes 101449728 | tf_op jit(solution)/shard_map/reduce_scatter | solution.py:208
  1464.2 12.2 copy-start.29
  1464.2 12.2 copy-start.30
  1464.2 12.2 copy-start.31
  1464.2 81.9 %copy-start.33 = (f32[128]{0:T(128)S(1)}, f32[128]{0:T(128)}, u32[]{:S(2)}) copy-start(f32[128]{0:T(128)} %copy-done.32) | copy-start | bytes 1540
  1464.2 81.9 %copy-start.11 = (f32[128,2048]{1,0:T(8,128)S(1)}, f32[128,2048]{1,0:T(8,128)}, u32[]{:S(2)}) copy-start(f32[128,2048]{1,0:T(8,128)} %copy-done.10) | copy-start | bytes 3145732
Sparse Core Ops, SparseCore 0:
  9.7 216.6 all-gather.6
  235.7 54.8 all-gather.8
  293.5 54.5 all-gather.10
  349.7 200.0 all-gather.12
  551.3 278.3 all-gather.14
  831.3 228.1 all-gather.16
  1166.3 77.9 reduce-scatter.20
  1248.8 79.3 reduce-scatter.18
  1331.1 658.5 reduce-scatter.14
  1992.6 686.7 reduce-scatter.12
  2682.3 715.3 reduce-scatter.22
  3400.6 799.6 reduce-scatter.16
where the time goes:
time: 4220 us; the launch traced here: 4210 us
  waiting for transfers between devices  3650 us (86%)
  matrix products  282 us (7%)
  blocking collectives  136 us (3%)
  local copies, waits for them, and re-layouts  93.2 us (2%)
    unnamed x15, waiting for transfers between devices  806 us
    reduce_scatter x1, waiting for transfers between devices, local(): lax.psum_scatter(contract_first(normed_m, joined_grad), ('dp', 'fsdp'), s...  803 us
    reduce_scatter x1, waiting for transfers between devices, local(): lax.psum_scatter(contract_first(normed, projected_low), ('dp', 'fsdp'), s...  690 us
    reduce_scatter x1, waiting for transfers between devices, local(): lax.psum_scatter(out_term, ('dp', 'fsdp'), scatter_dimension=0, tiled=True)  442 us
    all_gather x1, waiting for transfers between devices, local(): lax.all_gather(gate_up_weight, ('dp', 'fsdp'), axis=0, tiled=True)  274 us
    all_gather x1, waiting for transfers between devices, local(): lax.all_gather(down_weight, ('dp', 'fsdp'), axis=0, tiled=True)  209 us
    all_gather x1, waiting for transfers between devices, local(): lax.all_gather(out_weight, ('dp', 'fsdp'), axis=0, tiled=True)  188 us
    all_gather x1, waiting for transfers between devices, local(): lax.all_gather(qkv_weight, ('dp', 'fsdp'), axis=0, tiled=True)  145 us
  transfers between devices with their start and end apart: 12, of which 12 were waited for; matrix products, arithmetic and copies ran while one was open for 7% of the time, Pallas kernels for 0%

commit v1 on v0

v1 whole, which is shorter than its diff:
```python
import math

import jax
import jax.numpy as jnp
from jax import lax
from jax.experimental import pallas as pl
from jax.experimental.pallas import tpu as pltpu
from jax.sharding import Mesh
from jax.sharding import PartitionSpec as P

HEAD_SIZE = 128
FF = 6144
ROWS = 128
GROUP = 8
HALF_KEYS = ROWS * GROUP
KEYS = 2 * HALF_KEYS
SCALE = HEAD_SIZE**-0.5
EPS = 1e-6
ROPE_BASE = 1000000.0
AXES = ("x", "yl", "yh", "z", "c")
TP = ("z", "c")
PLANE = ("x", "yl", "yh")
f32 = jnp.float32
bf16 = jnp.bfloat16


def row_layout(seq_counts, device, token_rows):
    seq_ends = jnp.cumsum(seq_counts)
    starts = seq_ends - seq_counts
    row_place = jnp.arange(token_rows, dtype=jnp.int32)
    inside = (
        (row_place[:, None] >= starts[None, :]) & (row_place[:, None] < seq_ends[None, :])
    ).astype(jnp.int32)
    slot_ids = jnp.arange(seq_counts.shape[0], dtype=jnp.int32)
    in_sequence = row_place < seq_ends[-1]
    segment = jnp.where(in_sequence, jnp.sum(inside * slot_ids[None, :], axis=1), -1)
    length = jnp.sum(inside * seq_counts[None, :], axis=1)
    seq_begin = jnp.sum(inside * starts[None, :], axis=1)
    position = device * length[None, :] + row_place[None, :] - seq_begin[None, :]
    return (position, segment)


def rope_tables(position):
    half_dim = HEAD_SIZE // 2
    frequency = jnp.exp(
        jnp.arange(half_dim, dtype=f32) * (-2.0 * math.log(ROPE_BASE) / HEAD_SIZE)
    )
    angles = position.astype(f32)[:, None] * frequency[None, :]
    return (jnp.cos(angles)[:, None, :], jnp.sin(angles)[:, None, :])


def rotate(values, cosine, sine_part):
    half_dim = HEAD_SIZE // 2
    a = values[..., :half_dim]
    b = values[..., half_dim:]
    return jnp.concatenate(
        [a * cosine - b * sine_part, b * cosine + a * sine_part], axis=-1
    )


def rms_scale(values, gain):
    return values * lax.rsqrt(jnp.mean(values * values, axis=-1, keepdims=True) + EPS) * gain


def prepare(projected, q_gain, k_gain, cosine, sine_part):
    rows = projected.shape[0]
    q = projected[:, :256].reshape(rows, 2, HEAD_SIZE)
    k = projected[:, 256:384].reshape(rows, 1, HEAD_SIZE)
    q = rotate(rms_scale(q, q_gain), cosine, sine_part)
    k = rotate(rms_scale(k, k_gain), cosine, sine_part)
    return q, k[:, 0], projected[:, 384:]


def swiglu(joined):
    half = joined.shape[1] // 2
    return jax.nn.silu(joined[:, :half]) * joined[:, half:]


def dot(a, b):
    return jnp.dot(a, b, preferred_element_type=f32)


def dot_nt(a, b):
    return lax.dot_general(a, b, (((1,), (1,)), ((), ())), preferred_element_type=f32)


def dot_tn(a, b):
    return lax.dot_general(a, b, (((0,), (0,)), ((), ())), preferred_element_type=f32)


MESH = pl.DeviceIdType.MESH
HALF = 64
ANY = pl.BlockSpec(memory_space=pl.ANY)
VM = pl.BlockSpec(memory_space=pltpu.VMEM)

def where():
    z = lax.axis_index("z"); c = lax.axis_index("c")
    return z, c, lax.rem(z + 1, 4), lax.rem(z + 3, 4), lax.rem(z + 2, 4)

def greet(z, c, up, dn):
    b = pltpu.get_barrier_semaphore()
    pl.semaphore_signal(b, inc=1, device_id={"z": up}, device_id_type=MESH)
    pl.semaphore_signal(b, inc=1, device_id={"z": dn}, device_id_type=MESH)
    pl.semaphore_signal(b, inc=1, device_id={"c": 1 - c}, device_id_type=MESH)
    pl.semaphore_wait(b, 3)

def ag_kernel(x_ref, o_ref, own_sem, send, recv):
    z, c, up, dn, far = where()
    greet(z, c, up, dn)
    me = 2 * z + c
    own = pltpu.make_async_copy(x_ref, o_ref.at[me], own_sem)
    own.start()
    A, B = pl.ds(0, HALF), pl.ds(HALF, HALF)
    def rc(src, dst, i, to):
        return pltpu.make_async_remote_copy(src, dst, send.at[i], recv.at[i], device_id=to, device_id_type=MESH)
    UP, DN, SIB = {"z": up}, {"z": dn}, {"c": 1 - c}
    s_dn, s_up, s_far = 2 * dn + c, 2 * up + c, 2 * far + c
    cp = [
        rc(x_ref.at[A], o_ref.at[me, A], 0, UP),
        rc(x_ref.at[B], o_ref.at[me, B], 1, UP),
        rc(o_ref.at[s_dn, A], o_ref.at[s_dn, A], 2, UP),
        rc(x_ref.at[B], o_ref.at[me, B], 3, DN),
        rc(x_ref.at[A], o_ref.at[me, A], 4, DN),
        rc(o_ref.at[s_up, B], o_ref.at[s_up, B], 5, DN),
        rc(x_ref, o_ref.at[me], 6, SIB),
        rc(o_ref.at[s_dn], o_ref.at[s_dn], 7, SIB),
        rc(o_ref.at[s_up], o_ref.at[s_up], 8, SIB),
        rc(o_ref.at[s_far, A], o_ref.at[s_far, A], 9, SIB),
        rc(o_ref.at[s_far, B], o_ref.at[s_far, B], 10, SIB),
    ]
    for i in (0, 3, 1, 4, 6):
        cp[i].start()
    cp[0].wait_recv(); cp[2].start()
    cp[3].wait_recv(); cp[5].start()
    cp[1].wait_recv(); cp[7].start()
    cp[4].wait_recv(); cp[8].start()
    cp[2].wait_recv(); cp[9].start()
    cp[5].wait_recv(); cp[10].start()
    for i in (6, 7, 8, 9, 10):
        cp[i].wait_recv()
    for i in range(11):
        cp[i].wait_send()
    own.wait()

def ag(x, cid=0):
    return pl.pallas_call(
        ag_kernel, out_shape=jax.ShapeDtypeStruct((8, ROWS) + x.shape[1:], x.dtype),
        in_specs=[ANY], out_specs=ANY,
        scratch_shapes=[pltpu.SemaphoreType.DMA, pltpu.SemaphoreType.DMA((11,)), pltpu.SemaphoreType.DMA((11,))],
        compiler_params=pltpu.CompilerParams(collective_id=cid, has_side_effects=True, vmem_limit_bytes=32<<20),
    )(x)

def rs_kernel(p_ref, o_ref, sib_in, acc, in_up, in_dn, fwd, send, recv):
    z, c, up, dn, far = where()
    greet(z, c, up, dn)
    A, B = pl.ds(0, HALF), pl.ds(HALF, HALF)
    def rc(src, dst, i, to):
        return pltpu.make_async_remote_copy(src, dst, send.at[i], recv.at[i], device_id=to, device_id_type=MESH)
    UP, DN, SIB = {"z": up}, {"z": dn}, {"c": 1 - c}
    order = (far, up, dn, z)
    sib = [rc(p_ref.at[2 * zz + 1 - c], sib_in.at[k], k, SIB) for k, zz in enumerate(order)]
    for s in sib:
        s.start()
    def add(k):
        sib[k].wait_recv()
        acc[k] = (p_ref[2 * order[k] + c].astype(f32) + sib_in[k].astype(f32)).astype(bf16)
    cp = [
        rc(acc.at[0, A], fwd.at[0], 4, DN),
        rc(acc.at[0, B], fwd.at[1], 5, UP),
        rc(acc.at[1, A], in_dn.at[A], 6, UP),
        rc(acc.at[1, B], in_dn.at[B], 7, UP),
        rc(acc.at[2, B], in_up.at[B], 8, DN),
        rc(acc.at[2, A], in_up.at[A], 9, DN),
    ]
    add(0); cp[0].start(); cp[1].start()
    add(1); cp[2].start()
    add(2); cp[4].start()
    cp[1].wait_recv()
    acc[1, B] = (acc[1, B].astype(f32) + fwd[1].astype(f32)).astype(bf16)
    cp[3].start()
    cp[0].wait_recv()
    acc[2, A] = (acc[2, A].astype(f32) + fwd[0].astype(f32)).astype(bf16)
    cp[5].start()
    sib[3].wait_recv()
    o_ref[...] = p_ref[2 * z + c].astype(f32) + sib_in[3].astype(f32)
    cp[2].wait_recv(); cp[3].wait_recv(); cp[4].wait_recv(); cp[5].wait_recv()
    o_ref[...] += in_up[...].astype(f32) + in_dn[...].astype(f32)
    for s in sib + cp:
        s.wait_send()

def rs(p, cid=1):
    n = p.shape[-1]
    return pl.pallas_call(
        rs_kernel, out_shape=jax.ShapeDtypeStruct((ROWS, n), f32),
        in_specs=[VM], out_specs=VM,
        scratch_shapes=[pltpu.VMEM((4, ROWS, n), bf16), pltpu.VMEM((4, ROWS, n), bf16), pltpu.VMEM((ROWS, n), bf16), pltpu.VMEM((ROWS, n), bf16), pltpu.VMEM((2, HALF, n), bf16),
            pltpu.SemaphoreType.DMA((10,)), pltpu.SemaphoreType.DMA((10,))],
        compiler_params=pltpu.CompilerParams(collective_id=cid, has_side_effects=True, vmem_limit_bytes=48<<20),
    )(p)


def gather_rows(a):
    return ag(a).reshape(HALF_KEYS, a.shape[1])


def scatter_rows(a):
    return rs(a.astype(bf16).reshape(GROUP, ROWS, a.shape[1]))


def gather_weight(a):
    return lax.all_gather(a, PLANE, axis=0, tiled=True)


def scatter_weight(a):
    return lax.psum_scatter(a.astype(bf16), PLANE, scatter_dimension=0, tiled=True)


def swap(a):
    return lax.all_to_all(a, TP, split_axis=0, concat_axis=0, tiled=True)


def norm_back(g, xhat, rstd):
    return rstd * (g - xhat * jnp.mean(g * xhat, axis=-1, keepdims=True))


def chunks(w, parts):
    pieces = []
    at = 0
    for width in parts:
        pieces.append(w[:, at : at + width * GROUP].reshape(16, GROUP, width))
        at += width * GROUP
    return jnp.concatenate(pieces, axis=2)


def unchunk(g, parts):
    pieces = []
    at = 0
    for width in parts:
        pieces.append(g[:, :, at : at + width].transpose(1, 0, 2).reshape(16, GROUP * width))
        at += width
    return jnp.concatenate(pieces, axis=1)


def local(
    tokens,
    cotangent,
    seq_rows,
    qkv_weight,
    out_weight,
    attn_gain,
    query_gain,
    key_gain,
    gate_up_weight,
    down_weight,
    mlp_gain,
):
    yh = lax.axis_index("yh")
    gain_a = attn_gain.astype(f32)[:, None]
    gain_m = mlp_gain.astype(f32)[:, None]
    qkv_f = qkv_weight.astype(f32)
    gate_up_f = gate_up_weight.astype(f32)
    pieces = jnp.concatenate(
        [
            chunks((qkv_f * gain_a).astype(bf16), (256, 128, 128)),
            chunks(out_weight, (256,)),
            chunks((gate_up_f * gain_m).astype(bf16), (768, 768)),
            chunks(down_weight, (768,)),
        ],
        axis=2,
    ).transpose(1, 0, 2)
    mine = swap(pieces).reshape(ROWS, 3072)
    w_qkv = gather_weight(mine[:, :512])
    w_out = gather_weight(mine[:, 512:768])
    w_gate_up = gather_weight(mine[:, 768:2304])
    w_down = gather_weight(mine[:, 2304:])
    gains = lax.all_gather(
        jnp.concatenate([query_gain, key_gain])[None], AXES, axis=0, tiled=True
    ).astype(f32)
    gain_q, gain_k = gains[:, 0], gains[:, 1]

    counts = seq_rows[0]
    position_all, segment = row_layout(counts, jnp.arange(16, dtype=jnp.int32)[:, None], ROWS)
    key_position = position_all.reshape(KEYS)
    own_position = lax.dynamic_slice_in_dim(key_position, yh * HALF_KEYS, HALF_KEYS)
    key_segment = jnp.tile(segment, 16)
    own_segment = jnp.tile(segment, 8)
    query_index = yh * HALF_KEYS + jnp.arange(HALF_KEYS, dtype=jnp.int32)
    key_index = jnp.arange(KEYS, dtype=jnp.int32)
    visible = (own_segment[:, None] == key_segment[None, :]) & (own_segment[:, None] >= 0) & (
        key_position[None, :] <= own_position[:, None]
    ) | (query_index[:, None] == key_index[None, :])
    cosine, sine_part = rope_tables(own_position)

    x = tokens.astype(f32)
    rstd = lax.rsqrt(jnp.mean(x * x, axis=-1, keepdims=True) + EPS)
    xhat = x * rstd
    n_full = gather_rows(xhat.astype(bf16))
    c_full = gather_rows(cotangent)
    projected = dot(n_full, w_qkv)

    def prepare_local(p, gq, gk):
        return prepare(p, gq, gk, cosine, sine_part)

    (q, k, v), prepare_back = jax.vjp(prepare_local, projected, gain_q, gain_k)
    q = q.astype(bf16)
    kv = jnp.concatenate([k.astype(bf16), v.astype(bf16)], axis=1)
    kv_all = lax.all_gather(kv, "yh", axis=0, tiled=True)
    k_all, v_all = kv_all[:, :128], kv_all[:, 128:]
    scores = jnp.einsum("tnd,sd->nts", q, k_all, preferred_element_type=f32)
    scores = jnp.where(visible[None], scores * SCALE, -1e30)
    peak = jnp.max(scores, axis=-1, keepdims=True)
    lse = peak + jnp.log(jnp.sum(jnp.exp(scores - peak), axis=-1, keepdims=True))
    probs = jnp.exp(scores - lse).astype(bf16)
    attended = jnp.einsum("nts,sd->tnd", probs, v_all, preferred_element_type=f32)
    attended = attended.astype(bf16).reshape(HALF_KEYS, 256)
    middle = x + scatter_rows(dot_nt(attended, w_out))

    rstd_m = lax.rsqrt(jnp.mean(middle * middle, axis=-1, keepdims=True) + EPS)
    mhat = middle * rstd_m
    m_full = gather_rows(mhat.astype(bf16))
    joined = dot(m_full, w_gate_up)
    hidden_f, swiglu_back = jax.vjp(swiglu, joined)
    hidden = hidden_f.astype(bf16)
    block_out = (middle + scatter_rows(dot_nt(hidden, w_down))).astype(bf16)
    g_joined = swiglu_back(dot(c_full, w_down))[0].astype(bf16)
    g_mhat = scatter_rows(dot_nt(g_joined, w_gate_up))
    g_middle = cotangent.astype(f32) + norm_back(g_mhat, mhat, rstd_m)
    down_part = scatter_weight(dot_tn(c_full, hidden))
    gate_up_part = scatter_weight(dot_tn(m_full, g_joined))

    b_full = gather_rows(g_middle.astype(bf16))
    g_attended = dot(b_full, w_out).astype(bf16).reshape(HALF_KEYS, 2, HEAD_SIZE)
    out_part = scatter_weight(dot_tn(b_full, attended))
    probs_full = jnp.exp(scores - lse)
    g_probs = jnp.einsum("tnd,sd->nts", g_attended, v_all, preferred_element_type=f32)
    inner = jnp.sum(probs_full * g_probs, axis=-1, keepdims=True)
    g_raw = (probs_full * (g_probs - inner) * SCALE).astype(bf16)
    g_q = jnp.einsum("nts,sd->tnd", g_raw, k_all, preferred_element_type=f32)
    g_k = jnp.einsum("nts,tnd->sd", g_raw, q, preferred_element_type=f32)
    g_v = jnp.einsum(
        "nts,tnd->sd", probs_full.astype(bf16), g_attended, preferred_element_type=f32
    )
    g_kv = lax.psum_scatter(
        jnp.concatenate([g_k, g_v], axis=1).astype(bf16), "yh", scatter_dimension=0, tiled=True
    ).astype(f32)
    g_projected, g_gain_q, g_gain_k = prepare_back((g_q, g_kv[:, :128], g_kv[:, 128:]))
    g_projected = g_projected.astype(bf16)
    g_xhat = scatter_rows(dot_nt(g_projected, w_qkv))
    tokens_grad = g_middle + norm_back(g_xhat, xhat, rstd)
    qkv_part = scatter_weight(dot_tn(n_full, g_projected))

    parts = jnp.concatenate([qkv_part, out_part, gate_up_part, down_part], axis=1)
    owned = swap(parts.reshape(GROUP, 16, 3072)).astype(f32)
    qkv_raw = unchunk(owned[:, :, :512], (256, 128, 128))
    out_grad = unchunk(owned[:, :, 512:768], (256,))
    gate_up_raw = unchunk(owned[:, :, 768:2304], (768, 768))
    down_grad = unchunk(owned[:, :, 2304:], (768,))
    gain_grads = lax.psum_scatter(
        jnp.stack([g_gain_q, g_gain_k], axis=1), AXES, scatter_dimension=0, tiled=True
    )
    return (
        block_out,
        tokens_grad,
        qkv_raw * gain_a,
        out_grad,
        jnp.sum(qkv_raw * qkv_f, axis=1),
        gain_grads[:, 0],
        gain_grads[:, 1],
        gate_up_raw * gain_m,
        down_grad,
        jnp.sum(gate_up_raw * gate_up_f, axis=1),
    )


def solution(mesh):
    fine = Mesh(mesh.devices.reshape(4, 2, 2, 4, 2), AXES)
    rows2 = P(AXES, None)
    rows1 = P(AXES)
    return jax.shard_map(
        local,
        mesh=fine,
        in_specs=(
            rows2,
            rows2,
            P(("x", "yl"), None),
            rows2,
            rows2,
            rows1,
            rows1,
            rows1,
            rows2,
            rows2,
            rows1,
        ),
        out_specs=(
            rows2,
            rows2,
            rows2,
            rows2,
            rows1,
            rows1,
            rows1,
            rows2,
            rows2,
            rows1,
        ),
        check_vma=False,
    )
```

time: 4220 us -> 1040 us (0.25)
  waiting for transfers between devices: 3650 us -> 360 us
  Pallas kernels: 0 us -> 208 us
  matrix products: 282 us -> 165 us
  blocking collectives: 136 us -> 201 us
  local copies, waits for them, and re-layouts: 93.2 us -> 28.5 us
    reduce_scatter x3 -> x5, waiting for transfers between devices: 1930 us -> 177 us  [the longest x4 177 us: scatter_weight(): lax.psum_scatter(a.astype(bf16), PLANE, scatter_dimension=0, tiled=True)]
    unnamed x15 -> x10, waiting for transfers between devices: 806 us -> 0.16 us
    all_gather x6 -> x5, waiting for transfers between devices: 911 us -> 174 us  [the longest x4 174 us: gather_weight(): return lax.all_gather(a, PLANE, axis=0, tiled=True)]
    pallas_call x0 -> x8, Pallas kernels: none -> 208 us  [the longest x4 116 us: rs(): pl.pallas_call(rs_kernel, out_shape=jax.ShapeDtypeStruct((ROWS, n), f32),...]
    dot_general x36 -> x18, matrix products: 282 us -> 165 us  [the longest x4 30.2 us: dot(): return jnp.dot(a, b, preferred_element_type=f32)]
    unnamed x95 -> x101, local copies, waits for them, and re-layouts: 80.1 us -> 14.4 us
    unnamed x2, blocking collectives: 136 us -> 182 us
  transfers between devices with their start and end apart: 12 -> 11, of which waited for: 12 -> 6; matrix products, arithmetic and copies ran while one was open for 7% -> 13% of each run, Pallas kernels for 0% -> 15%
where the time goes in v1:
time: 1040 us; the launch traced here: 1030 us
  waiting for transfers between devices  360 us (35%)
  Pallas kernels  208 us (20%)
  blocking collectives  201 us (19%)
  matrix products  165 us (16%)
  other arithmetic  44.8 us (4%)
  local copies, waits for them, and re-layouts  28.5 us (3%)
  between operations  16.9 us (2%)
    unnamed x2, blocking collectives  182 us
    reduce_scatter x4, waiting for transfers between devices, scatter_weight(): lax.psum_scatter(a.astype(bf16), PLANE, scatter_dimension=0, tiled=True)  177 us
    all_gather x4, waiting for transfers between devices, gather_weight(): return lax.all_gather(a, PLANE, axis=0, tiled=True)  174 us
    pallas_call x4, Pallas kernels, rs(): pl.pallas_call(rs_kernel, out_shape=jax.ShapeDtypeStruct((ROWS, n), f32),...  116 us
    pallas_call x4, Pallas kernels, ag(): pl.pallas_call(ag_kernel, out_shape=jax.ShapeDtypeStruct((8, ROWS) + x.sh...  92 us
    dot_general x4, matrix products, dot(): return jnp.dot(a, b, preferred_element_type=f32)  30.2 us
    dot_general x4, matrix products, dot_tn(): lax.dot_general(a, b, (((0,), (0,)), ((), ())), preferred_element_type=f32)  28.8 us
    dot_general x1, matrix products, local(): g_q = jnp.einsum('nts,sd->tnd', g_raw, k_all, preferred_element_type=f32)  27.6 us
  transfers between devices with their start and end apart: 11, of which 6 were waited for; matrix products, arithmetic and copies ran while one was open for 13% of the time, Pallas kernels for 15%

profile of v1, /device:TPU:1, one launch (start us, length us, event | category | flops | bytes accessed | tf_op | source)
XLA Modules:
  0.0 1030.2 jit_solution(5483579268695017573)
XLA Ops:
  12.0 1.1 fusion.24
  13.9 18.8 %all_to_all.10 = bf16[8,16,3072]{2,1,0:T(8,128)(2,1)S(1)} all-to-all(bf16[8,16,3072]{2,1,0:T(8,128)(2,1)S(1)} %copy.111), channel_id=1, replica_groups=mesh['x'=4,'yl'=2,'yh'=2,'z'=4,'c'=2] {'z','c'}, dimensions={0} | all-to-all | bytes 1572864 | tf_op jit(solution)/shard_map/all_to_all | solution.py:219
  36.1 76.1 %all-reduce.9 = bf16[256]{0:T(256)(128)(2,1)S(1)} all-reduce(bf16[256]{0:T(256)(128)(2,1)S(1)} %dynamic-update-slice), channel_id=2, replica_groups=mesh['x'=4,'yl'=2,'yh'=2,'z'=4,'c'=2] {'x','yl','yh','z','c'}, use_global_device_ids=true, to_apply=%add.9 | all-reduce | flops 256 | bytes 1024
  112.7 23.3 %shard_map.186 = bf16[8,128,2048]{2,1,0:T(8,128)(2,1)S(1)} custom-call(bf16[128,2048]{1,0:T(8,128)(2,1)S(1)} %fusion.17.x_ref), custom_call_target="tpu_custom_call" | custom-call | tf_op jit(solution)/shard_map/pallas_call | solution.py:146
  136.0 2.0 copy-done.2
  138.4 5.2 fusion.70
  143.9 1.2 fusion.42
  146.0 1.5 slice.162
  147.5 1.8 slice.163
  150.0 22.8 %shard_map.190 = bf16[8,128,2048]{2,1,0:T(8,128)(2,1)S(1)} custom-call(bf16[128,2048]{1,0:T(8,128)(2,1)S(1)} %copy-done), custom_call_target="tpu_custom_call" | custom-call | tf_op jit(solution)/shard_map/pallas_call | solution.py:146
  172.8 1.9 copy-done.5
  175.4 3.1 multiply_cosine_fusion
  178.5 4.2 fusion.6
  182.7 1.6 slice.166
  185.5 1.6 copy.112
  187.4 2.6 subtract_convert_fusion
  190.1 6.1 fusion.5
  196.3 4.0 exponential_reduce_fusion
  200.3 1.9 copy-done.10
  202.2 8.7 convolution_convert_fusion.9
  210.9 22.0 %all-gather.11.cloned.1.call-done = bf16[2048,256]{1,0:T(8,128)(2,1)} async-done(((bf16[128,256]{1,0:T(8,128)(2,1)}), bf16[2048,256]{1,0:T(8,128)(2,1)}) %all-gather.11.cloned.1.call-update) | async-done | bytes 1048592 | tf_op jit(solution)/shard_map/all_gather | solution.py:211
  232.9 2.5 convolution_convert_fusion.3
  235.5 34.9 %shard_map.187 = f32[128,2048]{1,0:T(8,128)S(1)} custom-call(bf16[8,128,2048]{2,1,0:T(8,128)(2,1)S(1)} %bitcast.209), custom_call_target="tpu_custom_call" | custom-call | tf_op jit(solution)/shard_map/pallas_call | solution.py:193
  270.8 22.9 %shard_map.188 = bf16[8,128,2048]{2,1,0:T(8,128)(2,1)S(1)} custom-call(bf16[128,2048]{1,0:T(8,128)(2,1)S(1)} %multiply_convert_fusion.1.x_ref), custom_call_target="tpu_custom_call" | custom-call | tf_op jit(solution)/shard_map/pallas_call | solution.py:146
  293.8 1.9 copy-done.4
  295.7 87.7 %all-gather.13.cloned.1.call-done = bf16[2048,1536]{1,0:T(8,128)(2,1)} async-done(((bf16[128,1536]{1,0:T(8,128)(2,1)}), bf16[2048,1536]{1,0:T(8,128)(2,1)}) %all-gather.13.cloned.1.call-update) | async-done | bytes 6291472 | tf_op jit(solution)/shard_map/all_gather | solution.py:211
  383.4 12.1 %fusion.71 = f32[1024,1536]{1,0:T(8,128)} fusion(bf16[1024,2048]{1,0:T(8,128)(2,1)} %bitcast.215, bf16[2048,1536]{1,0:T(8,128)(2,1)} %all-gather.13.cloned.1.call-done), kind=kOutput, calls=%fused_computation.180 | convolution fusion | flops 6442450944 | bytes 16777216 | tf_op jit(solution)/shard_map/dot_general | solution.py:80
  395.5 64.5 %all-gather.15.cloned.1.call-done = bf16[2048,768]{1,0:T(8,128)(2,1)} async-done(((bf16[128,768]{1,0:T(8,128)(2,1)}), bf16[2048,768]{1,0:T(8,128)(2,1)}) %all-gather.15.cloned.1.call-update) | async-done | bytes 3145744 | tf_op jit(solution)/shard_map/all_gather | solution.py:211
  460.0 11.5 %bitcast_multiply_fusion.2 = (f32[1024,768]{1,0:T(8,128)S(1)}, f32[1024,768]{1,0:T(8,128)}, bf16[1024,768]{1,0:T(8,128)(2,1)}) fusion(f32[1024,1536]{1,0:T(8,128)} %fusion.71, bf16[1024,2048]{1,0:T(8,128)(2,1)} %bitcast.217, bf16[2048,768]{1,0:T(8,128)(2,1)} %all-gather.15.cloned.1.call-done), kind=kOutput, calls=%fused_computation.24 | convolution fusion | flops 3232235520 | bytes 21495808 | tf_op jit(solution)/shard_map/dot_general | solution.py:80
  471.6 9.5 convolution_convert_fusion.1
  481.1 34.4 %shard_map.191 = f32[128,2048]{1,0:T(8,128)S(1)} custom-call(bf16[8,128,2048]{2,1,0:T(8,128)(2,1)S(1)} %bitcast.212), custom_call_target="tpu_custom_call" | custom-call | tf_op jit(solution)/shard_map/pallas_call | solution.py:193
  516.2 22.9 %shard_map.192 = bf16[8,128,2048]{2,1,0:T(8,128)(2,1)S(1)} custom-call(bf16[128,2048]{1,0:T(8,128)(2,1)S(1)} %fusion.64.x_ref), custom_call_target="tpu_custom_call" | custom-call | tf_op jit(solution)/shard_map/pallas_call | solution.py:146
  539.1 1.3 convolution_convert_fusion.8
  542.2 8.9 fusion.12
  551.2 8.1 fusion.29
  559.3 26.3 %fusion.11 = bf16[2048,128]{0,1:T(8,128)(2,1)} fusion(f32[2048,1024,2]{1,0,2:T(8,128)} %fusion.29, f32[2048,1024,2]{1,0,2:T(8,128)} %copy-done.10, f32[2,1024]{1,0:T(2,128)S(1)} %log_add_fusion, pred[1024,2048]{0,1:T(8,128)(4,1)} %fusion.6, bf16[1024,2,64]{2,0,1:T(8,128)(2,1)} %get-tuple-element.27, bf16[1024,2,64]{2,0,1:T(8,128)(2,1)} %get-tuple-element.26), kind=kOutput, calls=%fused_computation.33 | convolution fusion | flops 1121193984 | bytes 36708352 | tf_op jit(solution)/shard_map/nts,tnd->sd/dot_general | solution.py:339
  585.6 2.1 pad_maximum_fusion
  587.7 4.5 convolution_convert_fusion.7
  592.3 8.1 fusion.10
  600.6 27.6 %fusion.18 = f32[1024,2,128]{2,0,1:T(8,128)} fusion(f32[2048,1024,2]{1,0,2:T(8,128)} %fusion.29, f32[2048,1024,2]{1,0,2:T(8,128)} %copy-done.10, f32[2,1024]{1,0:T(2,128)S(1)} %log_add_fusion, pred[1024,2048]{0,1:T(8,128)(4,1)} %fusion.6, bf16[2048,256]{0,1:T(8,128)(2,1)} %all-gather.9.cloned.1.call-done), kind=kOutput, calls=%fused_computation.45 | convolution fusion | flops 1119883264 | bytes 72892416 | tf_op jit(solution)/shard_map/nts,sd->tnd/dot_general | solution.py:338
  628.2 2.0 multiply_add_fusion.1
  632.2 1.3 copy.125
  633.5 1.1 slice.167
  634.7 1.8 convert_element_type.133
  636.5 1.2 fusion.45
  637.7 1.2 fusion.27
  638.9 1.2 fusion.26
  640.9 3.7 convolution_convert_fusion.6
  644.7 12.4 %convolution_convert_fusion = bf16[2048,1536]{1,0:T(8,128)(2,1)} fusion(bf16[1024,2048]{1,0:T(8,128)(2,1)} %bitcast.216, f32[1024,768]{1,0:T(8,128)} %get-tuple-element.22, f32[1024,768]{1,0:T(8,128)} %copy-done.38), kind=kOutput, calls=%fused_computation.13 | convolution fusion | flops 6448742400 | bytes 16777216 | tf_op jit(solution)/shard_map/dot_general | solution.py:88
  657.1 5.8 convolution_convert_fusion.4
  663.0 23.0 %shard_map.189 = f32[128,2048]{1,0:T(8,128)S(1)} custom-call(bf16[8,128,2048]{2,1,0:T(8,128)(2,1)S(1)} %bitcast.211), custom_call_target="tpu_custom_call" | custom-call | tf_op jit(solution)/shard_map/pallas_call | solution.py:193
  686.1 2.4 convolution_convert_fusion.2
  688.5 23.3 %shard_map.193 = f32[128,2048]{1,0:T(8,128)S(1)} custom-call(bf16[8,128,2048]{2,1,0:T(8,128)(2,1)S(1)} %bitcast.210), custom_call_target="tpu_custom_call" | custom-call | tf_op jit(solution)/shard_map/pallas_call | solution.py:193
  711.8 106.1 %all-reduce.10 = f32[128,2]{0,1:T(2,128)S(1)} all-reduce(f32[128,2]{0,1:T(2,128)S(1)} %pad_maximum_fusion.6), channel_id=8, replica_groups=mesh['x'=4,'yl'=2,'yh'=2,'z'=4,'c'=2] {'x','yl','yh','z','c'}, use_global_device_ids=true, to_apply=%region_23.24.clone | all-reduce | flops 256 | bytes 2048
  818.0 1.3 fusion.19
  819.4 28.2 %reduce-scatter.9.cloned.1.call-done = bf16[128,512]{1,0:T(8,128)(2,1)} async-done(((bf16[2048,512]{1,0:T(8,128)(2,1)}), bf16[128,512]{1,0:T(8,128)(2,1)}) %reduce-scatter.9.cloned.1.call-update) | async-done | bytes 131088 | tf_op jit(solution)/shard_map/reduce_scatter | solution.py:215
  847.6 148.7 %reduce-scatter.13.cloned.1.call-done = bf16[128,1536]{1,0:T(8,128)(2,1)} async-done(((bf16[2048,1536]{1,0:T(8,128)(2,1)}), bf16[128,1536]{1,0:T(8,128)(2,1)}) %reduce-scatter.13.cloned.1.call-update) | async-done | bytes 393232 | tf_op jit(solution)/shard_map/reduce_scatter | solution.py:215
  996.3 2.1 pad_maximum_fusion.1
  998.4 6.0 all-to-all-start.1
  1004.9 3.3 fusion.22
  1008.2 8.6 all-to-all-done.1
  1016.8 1.3 convert_element_type.141
  1019.8 1.4 fusion.40
  1021.3 1.6 fusion.25
  (180 shorter events, 20.7 us)
Async XLA Ops:
  7.2 131.2 %all-gather.7.cloned.1.call-start = ((), (), s32[]{:S(2)}) async-start(), calls=%async_computation.7 | async-start | bytes 2228224 | tf_op jit(solution)/shard_map/all_gather | solution.py:211
  7.9 0.5 copy-start.31
  9.4 26.2 %copy-start.35 = (s32[1,2]{1,0:T(1,128)S(1)}, s32[1,2]{1,0:T(1,128)}, u32[]{:S(2)}) copy-start(s32[1,2]{1,0:T(1,128)} %param.13) | copy-start | bytes 28
  10.1 3.1 copy-start.33
  10.1 102.3 %copy-start.7 = (bf16[128,2048]{1,0:T(8,128)(2,1)S(1)}, bf16[128,2048]{1,0:T(8,128)(2,1)}, u32[]{:S(2)}) copy-start(bf16[128,2048]{1,0:T(8,128)(2,1)} %param.11) | copy-start | bytes 1572868
  32.7 0.9 copy-start.16
  34.3 155.8 %all-gather.9.cloned.1.call-start = ((), (), s32[]{:S(2)}) async-start(), calls=%async_computation.8 | async-start | bytes 1572864 | tf_op jit(solution)/shard_map/all_gather | solution.py:307
  112.5 25.8 %copy-start.29 = (f32[128]{0:T(128)}, f32[128]{0:T(128)S(1)}, u32[]{:S(2)}) copy-start(f32[128]{0:T(128)S(1)} %add_rsqrt_fusion.1) | copy-start | bytes 1540
  136.0 2.1 copy-start.2
  143.6 40.8 %copy-start.11 = (f32[1024,512]{0,1:T(8,128)}, f32[1024,512]{0,1:T(8,128)S(1)}, u32[]{:S(2)}) copy-start(f32[1024,512]{0,1:T(8,128)S(1)} %fusion.70) | copy-start | bytes 6291460
  143.7 6.3 copy-start
  145.9 87.0 %all-gather.11.cloned.1.call-start = ((), (), s32[]{:S(2)}) async-start(), calls=%async_computation.9 | async-start | bytes 1114112 | tf_op jit(solution)/shard_map/all_gather | solution.py:211
  147.5 235.9 %all-gather.13.cloned.1.call-start = ((), (), s32[]{:S(2)}) async-start(), calls=%async_computation.10 | async-start | bytes 6684672 | tf_op jit(solution)/shard_map/all_gather | solution.py:211
  149.3 310.7 %all-gather.15.cloned.1.call-start = ((), (), s32[]{:S(2)}) async-start(), calls=%async_computation.11 | async-start | bytes 3342336 | tf_op jit(solution)/shard_map/all_gather | solution.py:211
  172.8 1.9 copy-start.5
  184.3 449.2 %reduce-scatter.7.cloned.1.call-start = ((), (), s32[]{:S(2)}) async-start(), calls=%async_computation.12 | async-start | bytes 1572864 | tf_op jit(solution)/shard_map/reduce_scatter | solution.py:343
  187.1 9.1 copy-start.8
  190.1 6.2 copy-start.12
  196.2 6.0 copy-start.10
  196.3 6.0 copy-start.27
  210.9 24.6 %copy-start.17 = (bf16[128,2,1024]{2,0,1:T(8,128)(2,1)}, bf16[128,2,1024]{2,0,1:T(8,128)(2,1)S(1)}, u32[]{:S(2)}) copy-start(bf16[128,2,1024]{2,0,1:T(8,128)(2,1)S(1)} %convolution_convert_fusion.9) | copy-start | bytes 1572868
  293.7 2.0 copy-start.4
  460.0 11.5 %copy-start.36 = (bf16[2048,1536]{1,0:T(8,128)(2,1)S(1)}, bf16[2048,1536]{1,0:T(8,128)(2,1)}, u32[]{:S(2)}) copy-start(bf16[2048,1536]{1,0:T(8,128)(2,1)} %all-gather.13.cloned.1.call-done) | copy-start | bytes 18874372
  471.6 9.5 copy-start.38
  515.8 23.4 %copy-start.20 = (bf16[2048,256]{1,0:T(8,128)(2,1)S(1)}, bf16[2048,256]{1,0:T(8,128)(2,1)}, u32[]{:S(2)}) copy-start(bf16[2048,256]{1,0:T(8,128)(2,1)} %all-gather.11.cloned.1.call-done) | copy-start | bytes 3145732
  539.1 2.1 copy-start.6
  539.1 3.1 copy-start.13
  542.2 9.0 copy-start.28
  559.3 28.4 %copy-start.18 = (bf16[128,2,1024]{2,0,1:T(8,128)(2,1)S(1)}, bf16[128,2,1024]{2,0,1:T(8,128)(2,1)}, u32[]{:S(2)}) copy-start(bf16[128,2,1024]{2,0,1:T(8,128)(2,1)} %copy-done.17) | copy-start | bytes 1572868
  587.7 231.7 %reduce-scatter.11.cloned.1.call-start = ((), (), s32[]{:S(2)}) async-start(), calls=%async_computation.14 | async-start | bytes 1114112 | tf_op jit(solution)/shard_map/reduce_scatter | solution.py:215
  592.3 227.1 %reduce-scatter.15.cloned.1.call-start = ((), (), s32[]{:S(2)}) async-start(), calls=%async_computation.16 | async-start | bytes 3342336 | tf_op jit(solution)/shard_map/reduce_scatter | solution.py:215
  600.5 27.7 %copy-start.14 = (f32[1024,64]{1,0:T(8,128)S(1)}, f32[1024,64]{1,0:T(8,128)}, u32[]{:S(2)}) copy-start(f32[1024,64]{1,0:T(8,128)} %get-tuple-element.49) | copy-start | bytes 786436
  600.5 27.7 %copy-start.15 = (f32[1024,64]{1,0:T(8,128)S(1)}, f32[1024,64]{1,0:T(8,128)}, u32[]{:S(2)}) copy-start(f32[1024,64]{1,0:T(8,128)} %get-tuple-element.50) | copy-start | bytes 786436
  600.5 247.1 %reduce-scatter.9.cloned.1.call-start = ((), (), s32[]{:S(2)}) async-start(), calls=%async_computation.13 | async-start | bytes 2228224 | tf_op jit(solution)/shard_map/reduce_scatter | solution.py:215
  628.2 2.0 copy-start.9
  633.5 7.4 copy-start.21
  633.5 7.4 copy-start.3
  634.6 5.5 copy-start.23
  640.1 0.8 copy-start.25
  644.7 351.6 %reduce-scatter.13.cloned.1.call-start = ((), (), s32[]{:S(2)}) async-start(), calls=%async_computation.15 | async-start | bytes 6684672 | tf_op jit(solution)/shard_map/reduce_scatter | solution.py:215
  663.0 23.0 %copy-start.24 = (f32[1024,128]{0,1:T(8,128)S(1)}, f32[1024,128]{0,1:T(8,128)}, u32[]{:S(2)}) copy-start(f32[1024,128]{0,1:T(8,128)} %copy-done.23) | copy-start | bytes 1572868
  663.0 23.0 %copy-start.26 = (f32[1024,128]{0,1:T(8,128)S(1)}, f32[1024,128]{0,1:T(8,128)}, u32[]{:S(2)}) copy-start(f32[1024,128]{0,1:T(8,128)} %copy-done.25) | copy-start | bytes 1572868
  663.0 23.0 %copy-start.37 = (bf16[2048,512]{1,0:T(8,128)(2,1)S(1)}, bf16[2048,512]{1,0:T(8,128)(2,1)}, u32[]{:S(2)}) copy-start(bf16[2048,512]{1,0:T(8,128)(2,1)} %all-gather.7.cloned.1.call-done) | copy-start | bytes 6291460
  686.0 2.4 copy-start.1
  688.5 129.5 %copy-start.30 = (f32[128]{0:T(128)S(1)}, f32[128]{0:T(128)}, u32[]{:S(2)}) copy-start(f32[128]{0:T(128)} %copy-done.29) | copy-start | bytes 1540
  998.4 18.4 %all-to-all-start.1 = ((bf16[8,16,3072]{2,1,0:T(8,128)(2,1)}), bf16[8,16,3072]{2,1,0:T(8,128)(2,1)}, u32[]{:S(2)}, u32[]{:S(2)}) async-start(bf16[8,16,3072]{2,1,0:T(8,128)(2,1)} %bitcast.226), calls=%async_computation.6 | async-start | bytes 1572864 | tf_op jit(solution)/shard_map/all_to_all | solution.py:219
  1008.2 11.5 %copy-start.22 = (bf16[16,4096]{1,0:T(8,128)(2,1)S(1)}, bf16[16,4096]{1,0:T(8,128)(2,1)}, u32[]{:S(2)}) copy-start(bf16[16,4096]{1,0:T(8,128)(2,1)} %param.14) | copy-start | bytes 393220
  1008.2 11.6 %copy-start.32 = (f32[16]{0:T(128)S(1)}, f32[16]{0:T(128)}, u32[]{:S(2)}) copy-start(f32[16]{0:T(128)} %copy-done.31) | copy-start | bytes 196
  1018.1 3.2 copy-start.19
  1018.1 3.2 copy-start.34
Sparse Core Ops, SparseCore 0:
  34.4 67.8 all-gather.6
  146.1 20.8 all-gather.8
  169.2 63.6 all-gather.10
  235.0 148.3 all-gather.12
  385.5 74.4 all-gather.14
  587.8 21.0 reduce-scatter.6
  611.4 66.6 reduce-scatter.10
  680.5 83.6 reduce-scatter.14
  766.6 80.9 reduce-scatter.8
  849.9 146.3 reduce-scatter.12

commit v2 on v1

v2 whole, which is shorter than its diff:
```python
import math

import jax
import jax.numpy as jnp
from jax import lax
from jax.experimental import pallas as pl
from jax.experimental.pallas import tpu as pltpu
from jax.sharding import Mesh
from jax.sharding import PartitionSpec as P

HEAD_SIZE = 128
FF = 6144
ROWS = 128
GROUP = 8
HALF_KEYS = ROWS * GROUP
KEYS = 2 * HALF_KEYS
SCALE = HEAD_SIZE**-0.5
WIDTH = 3200
EPS = 1e-6
ROPE_BASE = 1000000.0
AXES = ("x", "yl", "yh", "z", "c")
TP = ("z", "c")
PLANE = ("x", "yl", "yh")
f32 = jnp.float32
bf16 = jnp.bfloat16


def row_layout(seq_counts, device, token_rows):
    seq_ends = jnp.cumsum(seq_counts)
    starts = seq_ends - seq_counts
    row_place = jnp.arange(token_rows, dtype=jnp.int32)
    inside = (
        (row_place[:, None] >= starts[None, :]) & (row_place[:, None] < seq_ends[None, :])
    ).astype(jnp.int32)
    slot_ids = jnp.arange(seq_counts.shape[0], dtype=jnp.int32)
    in_sequence = row_place < seq_ends[-1]
    segment = jnp.where(in_sequence, jnp.sum(inside * slot_ids[None, :], axis=1), -1)
    length = jnp.sum(inside * seq_counts[None, :], axis=1)
    seq_begin = jnp.sum(inside * starts[None, :], axis=1)
    position = device * length[None, :] + row_place[None, :] - seq_begin[None, :]
    return (position, segment)


def rope_tables(position):
    half_dim = HEAD_SIZE // 2
    frequency = jnp.exp(
        jnp.arange(half_dim, dtype=f32) * (-2.0 * math.log(ROPE_BASE) / HEAD_SIZE)
    )
    angles = position.astype(f32)[:, None] * frequency[None, :]
    return (jnp.cos(angles)[:, None, :], jnp.sin(angles)[:, None, :])


def rotate(values, cosine, sine_part):
    half_dim = HEAD_SIZE // 2
    a = values[..., :half_dim]
    b = values[..., half_dim:]
    return jnp.concatenate(
        [a * cosine - b * sine_part, b * cosine + a * sine_part], axis=-1
    )


def rms_scale(values, gain):
    return values * lax.rsqrt(jnp.mean(values * values, axis=-1, keepdims=True) + EPS) * gain


def prepare(projected, q_gain, k_gain, cosine, sine_part):
    rows = projected.shape[0]
    q = projected[:, :256].reshape(rows, 2, HEAD_SIZE)
    k = projected[:, 256:384].reshape(rows, 1, HEAD_SIZE)
    q = rotate(rms_scale(q, q_gain), cosine, sine_part)
    k = rotate(rms_scale(k, k_gain), cosine, sine_part)
    return q, k[:, 0], projected[:, 384:]


def swiglu(joined):
    half = joined.shape[1] // 2
    return jax.nn.silu(joined[:, :half]) * joined[:, half:]


def dot(a, b):
    return jnp.dot(a, b, preferred_element_type=f32)


def dot_nt(a, b):
    return lax.dot_general(a, b, (((1,), (1,)), ((), ())), preferred_element_type=f32)


def dot_tn(a, b):
    return lax.dot_general(a, b, (((0,), (0,)), ((), ())), preferred_element_type=f32)


MESH = pl.DeviceIdType.MESH
ANY = pl.BlockSpec(memory_space=pl.ANY)
VM = pl.BlockSpec(memory_space=pltpu.VMEM)
SM = pl.BlockSpec(memory_space=pltpu.SMEM)
HALF = 64
LOG2E = 1.4426950408889634


def params(cid=None, mib=56):
    if cid is None:
        return pltpu.CompilerParams(vmem_limit_bytes=mib << 20)
    return pltpu.CompilerParams(
        collective_id=cid, has_side_effects=True, vmem_limit_bytes=mib << 20
    )


def rcopy(src, dst, send, recv, to):
    return pltpu.make_async_remote_copy(
        src, dst, send, recv, device_id=to, device_id_type=MESH
    )


def ring_place():
    z, c = lax.axis_index("z"), lax.axis_index("c")
    return z, c, lax.rem(z + 1, 4), lax.rem(z + 3, 4), lax.rem(z + 2, 4)


def plane_place():
    return lax.axis_index("x"), lax.axis_index("yh") * 2 + lax.axis_index("yl")


def y_slot(y):
    return lax.rem(y, 2) * 2 + y // 2


def to_x(x):
    return {"x": x}


def to_y(y):
    return {"yl": lax.rem(y, 2), "yh": y // 2}


def to_group(j):
    return {"z": j // 2, "c": lax.rem(j, 2)}


def greet(targets):
    barrier = pltpu.get_barrier_semaphore()
    for to in targets:
        pl.semaphore_signal(barrier, inc=1, device_id=to, device_id_type=MESH)
    pl.semaphore_wait(barrier, len(targets))


def ring_targets():
    z, c, up, dn, far = ring_place()
    return [{"z": up}, {"z": dn}, {"c": 1 - c}]


def group_targets(me):
    return [to_group(lax.rem(me + d, GROUP)) for d in range(1, GROUP)]


def plane_targets(x, y):
    return [to_x(lax.rem(x + s, 4)) for s in (1, 2, 3)] + [
        to_y(lax.rem(y + s, 4)) for s in (1, 2, 3)
    ]


class RowGather:
    def __init__(self, src, dst, own_sem, send, recv):
        z, c, up, dn, far = ring_place()
        me = 2 * z + c
        low, high = pl.ds(0, HALF), pl.ds(HALF, HALF)
        s_dn, s_up, s_far = 2 * dn + c, 2 * up + c, 2 * far + c
        to_up, to_dn, to_sib = {"z": up}, {"z": dn}, {"c": 1 - c}
        plan = [
            (src.at[low], dst.at[me, low], to_up),
            (src.at[high], dst.at[me, high], to_up),
            (dst.at[s_dn, low], dst.at[s_dn, low], to_up),
            (src.at[high], dst.at[me, high], to_dn),
            (src.at[low], dst.at[me, low], to_dn),
            (dst.at[s_up, high], dst.at[s_up, high], to_dn),
            (src, dst.at[me], to_sib),
            (dst.at[s_dn], dst.at[s_dn], to_sib),
            (dst.at[s_up], dst.at[s_up], to_sib),
            (dst.at[s_far, low], dst.at[s_far, low], to_sib),
            (dst.at[s_far, high], dst.at[s_far, high], to_sib),
        ]
        self.cp = [rcopy(a, b, send.at[i], recv.at[i], to) for i, (a, b, to) in enumerate(plan)]
        self.own = pltpu.make_async_copy(src, dst.at[me], own_sem)

    def start(self):
        self.own.start()
        for i in (0, 3, 1, 4, 6):
            self.cp[i].start()

    def relay(self):
        cp = self.cp
        cp[0].wait_recv()
        cp[2].start()
        cp[3].wait_recv()
        cp[5].start()
        cp[1].wait_recv()
        cp[7].start()
        cp[4].wait_recv()
        cp[8].start()

    def have_own(self):
        self.own.wait()
        self.cp[6].wait_recv()

    def have_dn(self):
        self.cp[7].wait_recv()

    def have_up(self):
        self.cp[8].wait_recv()

    def have_far(self):
        cp = self.cp
        cp[2].wait_recv()
        cp[9].start()
        cp[5].wait_recv()
        cp[10].start()
        cp[9].wait_recv()
        cp[10].wait_recv()

    def drain(self):
        for c in self.cp:
            c.wait_send()


class Ring:
    def __init__(self, axis, at, block, first, rows, send, recv):
        step = to_x if axis == "x" else to_y
        up, dn = lax.rem(at + 1, 4), lax.rem(at + 3, 4)
        whole = pl.ds(first, rows)
        low, high = pl.ds(first, rows // 2), pl.ds(first + rows // 2, rows // 2)
        plan = [
            (block(at).at[whole], step(up)),
            (block(at).at[whole], step(dn)),
            (block(dn).at[low], step(up)),
            (block(up).at[high], step(dn)),
        ]
        self.cp = [rcopy(r, r, send.at[i], recv.at[i], to) for i, (r, to) in enumerate(plan)]

    def start(self):
        self.cp[0].start()
        self.cp[1].start()

    def relay(self):
        self.cp[0].wait_recv()
        self.cp[2].start()
        self.cp[1].wait_recv()
        self.cp[3].start()

    def finish(self):
        self.cp[2].wait_recv()
        self.cp[3].wait_recv()

    def drain(self):
        for c in self.cp:
            c.wait_send()


class PlaneGather:
    def __init__(self, dst, send, recv):
        x, y = plane_place()
        self.halves = []
        for half in (0, 1):
            first = half * HALF

            def along_x(y_at, x_at):
                return dst.at[x_at, y_slot(y_at)]

            def ring(axis, other, k):
                if axis == "x":
                    block = lambda at: dst.at[at, y_slot(other)]
                    at = x
                else:
                    block = lambda at: dst.at[other, y_slot(at)]
                    at = y
                return Ring(axis, at, block, first, HALF, send.at[half, k], recv.at[half, k])

            axes = ("y", "x") if half == 0 else ("x", "y")
            here, over = (y, x) if half == 0 else (x, y)
            others = [here, lax.rem(here + 3, 4), lax.rem(here + 1, 4), lax.rem(here + 2, 4)]
            self.halves.append(
                [ring(axes[0], over, 0)] + [ring(axes[1], o, 1 + k) for k, o in enumerate(others)]
            )

    def steps(self):
        a, b = self.halves

        def both(k, what):
            getattr(a[k], what)()
            getattr(b[k], what)()

        def one():
            both(0, "start")
            both(1, "start")

        def two():
            both(0, "relay")
            both(2, "start")
            both(3, "start")

        def three():
            both(1, "relay")
            both(0, "finish")
            both(4, "start")

        def four():
            both(2, "relay")
            both(3, "relay")

        def five():
            both(4, "relay")

        return [one, two, three, four, five]

    def finish(self):
        for half in self.halves:
            for k in range(1, 5):
                half[k].finish()
        for half in self.halves:
            for r in half:
                r.drain()


def front_kernel(x_ref, p_ref, n_ref, w_ref, own_sems, g_send, g_recv, s_send, s_recv, w_send, w_recv):
    z, c, up, dn, far = ring_place()
    me = 2 * z + c
    x, y = plane_place()
    greet(group_targets(me) + plane_targets(x, y))
    mine = w_ref.at[x, y_slot(y)]
    rows = pl.ds(pl.multiple_of(16 * me, 16), 16)
    own = pltpu.make_async_copy(p_ref.at[me], mine.at[rows], own_sems.at[0])
    own.start()
    swaps = []
    for d in range(1, GROUP):
        j = lax.rem(me + d, GROUP)
        swaps.append(rcopy(p_ref.at[j], mine.at[rows], s_send.at[d - 1], s_recv.at[d - 1], to_group(j)))
    for s in swaps:
        s.start()
    gather = RowGather(x_ref, n_ref, own_sems.at[1], g_send, g_recv)
    gather.start()
    own.wait()
    for s in swaps:
        s.wait_recv()
    plane = PlaneGather(w_ref, w_send, w_recv)
    steps = plane.steps()
    steps[0]()
    gather.relay()
    steps[1]()
    gather.have_own()
    gather.have_dn()
    gather.have_up()
    gather.have_far()
    for s in steps[2:]:
        s()
    plane.finish()
    gather.drain()
    for s in swaps:
        s.wait_send()


def front(xhat, pieces, cid):
    width = pieces.shape[2]
    dma = pltpu.SemaphoreType.DMA
    return pl.pallas_call(
        front_kernel,
        out_shape=(
            jax.ShapeDtypeStruct((GROUP, ROWS, xhat.shape[1]), bf16),
            jax.ShapeDtypeStruct((4, 4, ROWS, width), bf16),
        ),
        in_specs=[ANY, ANY],
        out_specs=(ANY, ANY),
        scratch_shapes=[
            dma((2,)),
            dma((11,)),
            dma((11,)),
            dma((7,)),
            dma((7,)),
            dma((2, 5, 4)),
            dma((2, 5, 4)),
        ],
        compiler_params=params(cid),
        name="front",
    )(xhat, pieces)


def grads_kernel(p_ref, o_ref, own_a, own_b, in_a, in_b, next_a, next_b, last, own_sems, send1, recv1, send2, recv2, s_send, s_recv):
    z, c, up, dn, far = ring_place()
    me = 2 * z + c
    x, y = plane_place()
    greet(group_targets(me) + plane_targets(x, y))
    low, high = pl.ds(0, HALF), pl.ds(HALF, HALF)
    first_a, first_b = [], []
    for s in (1, 2, 3):
        xt, yt = lax.rem(x + s, 4), lax.rem(y + s, 4)
        first_a.append(rcopy(p_ref.at[xt, :, low], in_a.at[s - 1], send1.at[0, s - 1], recv1.at[0, s - 1], to_x(xt)))
        first_b.append(rcopy(p_ref.at[:, y_slot(yt), high], in_b.at[s - 1], send1.at[1, s - 1], recv1.at[1, s - 1], to_y(yt)))
    for a, b in zip(first_a, first_b):
        a.start()
        b.start()
    get_a = pltpu.make_async_copy(p_ref.at[x, :, low], own_a, own_sems.at[0])
    get_b = pltpu.make_async_copy(p_ref.at[:, y_slot(y), high], own_b, own_sems.at[1])
    get_a.start()
    get_b.start()

    def total(own, arrived, k, r):
        t = own[k, r].astype(f32)
        for s in range(3):
            t += arrived[s, k, r].astype(f32)
        return t

    def sum_first(own, arrived):
        def body(i, carry):
            k, r = i // 4, pl.ds(pl.multiple_of(lax.rem(i, 4) * 16, 16), 16)
            own[k, r] = total(own, arrived, k, r).astype(bf16)
            return carry

        lax.fori_loop(0, 16, body, 0)

    get_a.wait()
    for a in first_a:
        a.wait_recv()
    sum_first(own_a, in_a)
    second_a, second_b = [], []
    for s in (1, 2, 3):
        yt, xt = lax.rem(y + s, 4), lax.rem(x + s, 4)
        second_a.append(rcopy(own_a.at[y_slot(yt)], next_a.at[s - 1], send2.at[0, s - 1], recv2.at[0, s - 1], to_y(yt)))
        second_b.append(rcopy(own_b.at[xt], next_b.at[s - 1], send2.at[1, s - 1], recv2.at[1, s - 1], to_x(xt)))
    for a in second_a:
        a.start()
    get_b.wait()
    for b in first_b:
        b.wait_recv()
    sum_first(own_b, in_b)
    for b in second_b:
        b.start()

    def sum_second(own, k, arrived, first):
        for i in range(4):
            r = pl.ds(16 * i, 16)
            t = own[k, r].astype(f32)
            for s in range(3):
                t += arrived[s, r].astype(f32)
            last[pl.ds(first + 16 * i, 16)] = t.astype(bf16)

    for a in second_a:
        a.wait_recv()
    sum_second(own_a, y_slot(y), next_a, 0)
    for b in second_b:
        b.wait_recv()
    sum_second(own_b, x, next_b, HALF)

    own = pltpu.make_async_copy(last.at[pl.ds(pl.multiple_of(16 * me, 16), 16)], o_ref.at[me], own_sems.at[2])
    own.start()
    swaps = []
    for d in range(1, GROUP):
        j = lax.rem(me + d, GROUP)
        swaps.append(rcopy(last.at[pl.ds(pl.multiple_of(16 * j, 16), 16)], o_ref.at[me], s_send.at[d - 1], s_recv.at[d - 1], to_group(j)))
    for s in swaps:
        s.start()
    own.wait()
    for s in swaps:
        s.wait_recv()
    for s in first_a + first_b + second_a + second_b + swaps:
        s.wait_send()


def scatter_grads(p, cid):
    width = p.shape[1]
    dma = pltpu.SemaphoreType.DMA
    return pl.pallas_call(
        grads_kernel,
        out_shape=jax.ShapeDtypeStruct((GROUP, 16, width), bf16),
        in_specs=[ANY],
        out_specs=ANY,
        scratch_shapes=[
            pltpu.VMEM((4, HALF, width), bf16),
            pltpu.VMEM((4, HALF, width), bf16),
            pltpu.VMEM((3, 4, HALF, width), bf16),
            pltpu.VMEM((3, 4, HALF, width), bf16),
            pltpu.VMEM((3, HALF, width), bf16),
            pltpu.VMEM((3, HALF, width), bf16),
            pltpu.VMEM((ROWS, width), bf16),
            dma((3,)),
            dma((2, 3)),
            dma((2, 3)),
            dma((2, 3)),
            dma((2, 3)),
            dma((7,)),
            dma((7,)),
        ],
        compiler_params=params(cid),
        name="grads",
    )(p.reshape(4, 4, ROWS, width))


def attend_kernel(late_ref, q_ref, kv_ref, okv_ref, qseg_ref, kseg_ref, o_ref, acc, tot):
    for h in range(2):
        cols = pl.ds(128 * h, 128)
        for i in range(4):
            rows = pl.ds(256 * i, 256)
            q = q_ref[rows, cols]
            t = jnp.zeros((256, 1), f32)
            a = jnp.zeros((256, 128), f32)
            for k in range(i + 1):
                keys = pl.ds(256 * k, 256)
                s = dot_nt(q, kv_ref[keys, 0:128])
                ok = qseg_ref[rows, :] == kseg_ref[0:1, keys]
                if k == i:
                    ok &= lax.broadcasted_iota(jnp.int32, (256, 256), 0) >= lax.broadcasted_iota(
                        jnp.int32, (256, 256), 1
                    )
                p = jnp.where(ok, jnp.exp2(s * (SCALE * LOG2E)), 0.0)
                t += jnp.sum(p, axis=1, keepdims=True)
                a += dot(p.astype(bf16), kv_ref[keys, 128:256])
            acc[rows, cols] = a
            tot[h, rows] = t

    @pl.when(late_ref[0] == 1)
    def _():
        for h in range(2):
            cols = pl.ds(128 * h, 128)

            def body(i, carry):
                rows = pl.ds(pl.multiple_of(256 * i, 256), 256)
                q = q_ref[rows, cols]
                t = tot[h, rows]
                a = acc[rows, cols]
                for k in range(4):
                    keys = pl.ds(256 * k, 256)
                    s = dot_nt(q, okv_ref[keys, 0:128])
                    ok = qseg_ref[rows, :] == kseg_ref[1:2, keys]
                    p = jnp.where(ok, jnp.exp2(s * (SCALE * LOG2E)), 0.0)
                    t += jnp.sum(p, axis=1, keepdims=True)
                    a += dot(p.astype(bf16), okv_ref[keys, 128:256])
                tot[h, rows] = t
                acc[rows, cols] = a
                return carry

            lax.fori_loop(0, 4, body, 0)

    for h in range(2):
        cols = pl.ds(128 * h, 128)
        o_ref[:, cols] = (acc[:, cols] / tot[h]).astype(bf16)


def attend(late, q, kv, okv, qseg, kseg):
    return pl.pallas_call(
        attend_kernel,
        out_shape=jax.ShapeDtypeStruct((HALF_KEYS, 256), bf16),
        in_specs=[SM, VM, VM, VM, VM, VM],
        out_specs=VM,
        scratch_shapes=[pltpu.VMEM((HALF_KEYS, 256), f32), pltpu.VMEM((2, HALF_KEYS, 1), f32)],
        compiler_params=params(),
        name="attend",
    )(late, q, kv, okv, qseg, kseg)


def attend_back_kernel(late_ref, q_ref, kv_ref, okv_ref, g_ref, qseg_ref, kseg_ref, gq_ref, gkv_ref, gokv_ref, ps, gps, tot, inn):
    gkv_ref[...] = jnp.zeros_like(gkv_ref)
    gokv_ref[...] = jnp.zeros_like(gokv_ref)

    def weigh(i, h, which, k, diagonal):
        rows, cols = pl.ds(256 * i, 256), pl.ds(128 * h, 128)
        source = okv_ref if which else kv_ref
        keys = pl.ds(pl.multiple_of(256 * k, 256), 256)
        slot = pl.ds(pl.multiple_of(256 * k + 1024 * which, 256), 256)
        s = dot_nt(source[keys, 0:128], q_ref[rows, cols])
        ok = kseg_ref[which, keys] == qseg_ref[0:1, rows]
        if diagonal:
            ok &= lax.broadcasted_iota(jnp.int32, (256, 256), 1) >= lax.broadcasted_iota(
                jnp.int32, (256, 256), 0
            )
        p = jnp.where(ok, jnp.exp2(s * (SCALE * LOG2E)), 0.0)
        gp = dot_nt(source[keys, 128:256], g_ref[rows, cols])
        tot[...] += jnp.sum(p, axis=0, keepdims=True)
        inn[...] += jnp.sum(p * gp, axis=0, keepdims=True)
        ps[slot] = p
        gps[slot] = gp

    def spread(i, h, which, k):
        rows, cols = pl.ds(256 * i, 256), pl.ds(128 * h, 128)
        source, out = (okv_ref, gokv_ref) if which else (kv_ref, gkv_ref)
        keys = pl.ds(pl.multiple_of(256 * k, 256), 256)
        slot = pl.ds(pl.multiple_of(256 * k + 1024 * which, 256), 256)
        p = ps[slot] * tot[...]
        ds = (p * (gps[slot] - inn[...]) * SCALE).astype(bf16)
        out[keys, 0:128] += dot(ds, q_ref[rows, cols])
        out[keys, 128:256] += dot(p.astype(bf16), g_ref[rows, cols])
        gq_ref[rows, cols] += dot_tn(ds, source[keys, 0:128])

    for h in range(2):
        for i in range(4):
            tot[...] = jnp.zeros_like(tot)
            inn[...] = jnp.zeros_like(inn)
            gq_ref[pl.ds(256 * i, 256), pl.ds(128 * h, 128)] = jnp.zeros((256, 128), f32)
            for k in range(i + 1):
                weigh(i, h, 0, k, k == i)

            @pl.when(late_ref[0] == 1)
            def _():
                def body(k, carry):
                    weigh(i, h, 1, k, False)
                    return carry

                lax.fori_loop(0, 4, body, 0)

            inv = 1.0 / tot[...]
            tot[...] = inv
            inn[...] = inn[...] * inv
            for k in range(i + 1):
                spread(i, h, 0, k)

            @pl.when(late_ref[0] == 1)
            def _():
                def body(k, carry):
                    spread(i, h, 1, k)
                    return carry

                lax.fori_loop(0, 4, body, 0)


def attend_back(late, q, kv, okv, g, qseg_row, kseg_col):
    return pl.pallas_call(
        attend_back_kernel,
        out_shape=tuple(jax.ShapeDtypeStruct((HALF_KEYS, 256), f32) for _ in range(3)),
        in_specs=[SM] + [VM] * 6,
        out_specs=(VM, VM, VM),
        scratch_shapes=[
            pltpu.VMEM((KEYS, 256), f32),
            pltpu.VMEM((KEYS, 256), f32),
            pltpu.VMEM((1, 256), f32),
            pltpu.VMEM((1, 256), f32),
        ],
        compiler_params=params(),
        name="attend_back",
    )(late, q, kv, okv, g, qseg_row, kseg_col)


def gather_kernel(x_ref, o_ref, own_sem, send, recv):
    greet(ring_targets())
    g = RowGather(x_ref, o_ref, own_sem, send, recv)
    g.start()
    g.relay()
    g.have_own()
    g.have_dn()
    g.have_up()
    g.have_far()
    g.drain()


def gather_rows(x, cid):
    dma = pltpu.SemaphoreType.DMA
    return pl.pallas_call(
        gather_kernel,
        out_shape=jax.ShapeDtypeStruct((GROUP, ROWS, x.shape[1]), x.dtype),
        in_specs=[ANY],
        out_specs=ANY,
        scratch_shapes=[dma, dma((11,)), dma((11,))],
        compiler_params=params(cid),
        name="gather_rows",
    )(x).reshape(HALF_KEYS, x.shape[1])


def rs_kernel(p_ref, o_ref, sib_in, acc, in_up, in_dn, fwd, send, recv):
    z, c, up, dn, far = ring_place()
    greet(ring_targets())
    A, B = pl.ds(0, HALF), pl.ds(HALF, HALF)
    def rc(src, dst, i, to):
        return pltpu.make_async_remote_copy(src, dst, send.at[i], recv.at[i], device_id=to, device_id_type=MESH)
    UP, DN, SIB = {"z": up}, {"z": dn}, {"c": 1 - c}
    order = (far, up, dn, z)
    sib = [rc(p_ref.at[2 * zz + 1 - c], sib_in.at[k], k, SIB) for k, zz in enumerate(order)]
    for s in sib:
        s.start()
    def add(k):
        sib[k].wait_recv()
        acc[k] = (p_ref[2 * order[k] + c].astype(f32) + sib_in[k].astype(f32)).astype(bf16)
    cp = [
        rc(acc.at[0, A], fwd.at[0], 4, DN),
        rc(acc.at[0, B], fwd.at[1], 5, UP),
        rc(acc.at[1, A], in_dn.at[A], 6, UP),
        rc(acc.at[1, B], in_dn.at[B], 7, UP),
        rc(acc.at[2, B], in_up.at[B], 8, DN),
        rc(acc.at[2, A], in_up.at[A], 9, DN),
    ]
    add(0); cp[0].start(); cp[1].start()
    add(1); cp[2].start()
    add(2); cp[4].start()
    cp[1].wait_recv()
    acc[1, B] = (acc[1, B].astype(f32) + fwd[1].astype(f32)).astype(bf16)
    cp[3].start()
    cp[0].wait_recv()
    acc[2, A] = (acc[2, A].astype(f32) + fwd[0].astype(f32)).astype(bf16)
    cp[5].start()
    sib[3].wait_recv()
    o_ref[...] = p_ref[2 * z + c].astype(f32) + sib_in[3].astype(f32)
    cp[2].wait_recv(); cp[3].wait_recv(); cp[4].wait_recv(); cp[5].wait_recv()
    o_ref[...] += in_up[...].astype(f32) + in_dn[...].astype(f32)
    for s in sib + cp:
        s.wait_send()

def scatter_rows(p, cid):
    n = p.shape[-1]
    p = p.astype(bf16).reshape(GROUP, ROWS, n)
    return pl.pallas_call(
        rs_kernel, out_shape=jax.ShapeDtypeStruct((ROWS, n), f32),
        in_specs=[VM], out_specs=VM,
        scratch_shapes=[pltpu.VMEM((4, ROWS, n), bf16), pltpu.VMEM((4, ROWS, n), bf16), pltpu.VMEM((ROWS, n), bf16), pltpu.VMEM((ROWS, n), bf16), pltpu.VMEM((2, HALF, n), bf16),
            pltpu.SemaphoreType.DMA((10,)), pltpu.SemaphoreType.DMA((10,))],
        compiler_params=pltpu.CompilerParams(collective_id=cid, has_side_effects=True, vmem_limit_bytes=48<<20),
    )(p)


def norm_back(g, xhat, rstd):
    return rstd * (g - xhat * jnp.mean(g * xhat, axis=-1, keepdims=True))


def chunks(w, parts):
    pieces = []
    at = 0
    for width in parts:
        pieces.append(w[:, at : at + width * GROUP].reshape(16, GROUP, width))
        at += width * GROUP
    return jnp.concatenate(pieces, axis=2)


def unchunk(g, parts):
    pieces = []
    at = 0
    for width in parts:
        pieces.append(g[:, :, at : at + width].transpose(1, 0, 2).reshape(16, GROUP * width))
        at += width
    return jnp.concatenate(pieces, axis=1)


def local(
    tokens,
    cotangent,
    seq_rows,
    qkv_weight,
    out_weight,
    attn_gain,
    query_gain,
    key_gain,
    gate_up_weight,
    down_weight,
    mlp_gain,
):
    yh = lax.axis_index("yh")
    gain_a = attn_gain.astype(f32)[:, None]
    gain_m = mlp_gain.astype(f32)[:, None]
    qkv_f = qkv_weight.astype(f32)
    gate_up_f = gate_up_weight.astype(f32)
    head_gains = jnp.broadcast_to(
        jnp.pad(jnp.concatenate([query_gain, key_gain]), (0, 126)), (16, GROUP, 128)
    )
    pieces = jnp.concatenate(
        [
            chunks((qkv_f * gain_a).astype(bf16), (256, 128, 128)),
            head_gains,
            chunks(out_weight, (256,)),
            chunks((gate_up_f * gain_m).astype(bf16), (768, 768)),
            chunks(down_weight, (768,)),
        ],
        axis=2,
    ).transpose(1, 0, 2)

    x = tokens.astype(f32)
    rstd = lax.rsqrt(jnp.mean(x * x, axis=-1, keepdims=True) + EPS)
    xhat = x * rstd
    n_full, weights = front(xhat.astype(bf16), pieces, 0)
    n_full = n_full.reshape(HALF_KEYS, 2048)
    weights = weights.reshape(2048, WIDTH)
    w_qkv = weights[:, :512]
    w_out = weights[:, 640:896]
    w_gate_up = weights[:, 896:2432]
    w_down = weights[:, 2432:]
    gain_q = weights[::16, 512].astype(f32)
    gain_k = weights[::16, 513].astype(f32)

    counts = seq_rows[0]
    position_all, segment = row_layout(counts, jnp.arange(16, dtype=jnp.int32)[:, None], ROWS)
    own_position = lax.dynamic_slice_in_dim(position_all.reshape(KEYS), yh * HALF_KEYS, HALF_KEYS)
    segment = jnp.tile(segment, 16)
    segment = jnp.where(segment < 0, 2 + jnp.arange(KEYS, dtype=jnp.int32), segment)
    own_segment = lax.dynamic_slice_in_dim(segment, yh * HALF_KEYS, HALF_KEYS)
    both_segments = jnp.stack([own_segment, segment[:HALF_KEYS]])
    late = yh.astype(jnp.int32).reshape(1)
    cosine, sine_part = rope_tables(own_position)

    c_full = gather_rows(cotangent, 1)
    projected = dot(n_full, w_qkv)

    def prepare_local(p, gq, gk):
        return prepare(p, gq, gk, cosine, sine_part)

    (q, k, v), prepare_back = jax.vjp(prepare_local, projected, gain_q, gain_k)
    q = q.astype(bf16).reshape(HALF_KEYS, 256)
    kv = jnp.concatenate([k.astype(bf16), v.astype(bf16)], axis=1)
    other_kv = lax.ppermute(kv, "yh", [(0, 1)])
    attended = attend(late, q, kv, other_kv, own_segment[:, None], both_segments)
    middle = x + scatter_rows(dot_nt(attended, w_out), 2)

    rstd_m = lax.rsqrt(jnp.mean(middle * middle, axis=-1, keepdims=True) + EPS)
    mhat = middle * rstd_m
    m_full = gather_rows(mhat.astype(bf16), 3)
    joined = dot(m_full, w_gate_up)
    hidden_f, swiglu_back = jax.vjp(swiglu, joined)
    hidden = hidden_f.astype(bf16)
    block_out = (middle + scatter_rows(dot_nt(hidden, w_down), 4)).astype(bf16)
    g_joined = swiglu_back(dot(c_full, w_down))[0].astype(bf16)
    g_mhat = scatter_rows(dot_nt(g_joined, w_gate_up), 5)
    g_middle = cotangent.astype(f32) + norm_back(g_mhat, mhat, rstd_m)
    down_part = dot_tn(c_full, hidden).astype(bf16)
    gate_up_part = dot_tn(m_full, g_joined).astype(bf16)

    b_full = gather_rows(g_middle.astype(bf16), 6)
    g_attended = dot(b_full, w_out).astype(bf16)
    out_part = dot_tn(b_full, attended).astype(bf16)
    g_q, g_kv, g_other_kv = attend_back(
        late, q, kv, other_kv, g_attended, own_segment[None], both_segments[:, :, None]
    )
    g_kv += lax.ppermute(g_other_kv.astype(bf16), "yh", [(1, 0)]).astype(f32)
    g_projected, g_gain_q, g_gain_k = prepare_back(
        (g_q.reshape(HALF_KEYS, 2, HEAD_SIZE), g_kv[:, :128], g_kv[:, 128:])
    )
    g_projected = g_projected.astype(bf16)
    g_xhat = scatter_rows(dot_nt(g_projected, w_qkv), 7)
    tokens_grad = g_middle + norm_back(g_xhat, xhat, rstd)
    qkv_part = dot_tn(n_full, g_projected).astype(bf16)
    gain_part = jnp.pad(
        jnp.stack([g_gain_q, g_gain_k], axis=1).astype(bf16)[:, None], ((0, 0), (0, 15), (0, 126))
    ).reshape(2048, 128)

    owned = scatter_grads(
        jnp.concatenate([qkv_part, gain_part, out_part, gate_up_part, down_part], axis=1), 8
    ).astype(f32)
    qkv_raw = unchunk(owned[:, :, :512], (256, 128, 128))
    gain_grads = jnp.sum(owned[:, 0, 512:514], axis=0)
    out_grad = unchunk(owned[:, :, 640:896], (256,))
    gate_up_raw = unchunk(owned[:, :, 896:2432], (768, 768))
    down_grad = unchunk(owned[:, :, 2432:], (768,))
    return (
        block_out,
        tokens_grad,
        qkv_raw * gain_a,
        out_grad,
        jnp.sum(qkv_raw * qkv_f, axis=1),
        gain_grads[:1],
        gain_grads[1:],
        gate_up_raw * gain_m,
        down_grad,
        jnp.sum(gate_up_raw * gate_up_f, axis=1),
    )


def solution(mesh):
    fine = Mesh(mesh.devices.reshape(4, 2, 2, 4, 2), AXES)
    rows2 = P(AXES, None)
    rows1 = P(AXES)
    return jax.shard_map(
        local,
        mesh=fine,
        in_specs=(
            rows2,
            rows2,
            P(("x", "yl"), None),
            rows2,
            rows2,
            rows1,
            rows1,
            rows1,
            rows2,
            rows2,
            rows1,
        ),
        out_specs=(
            rows2,
            rows2,
            rows2,
            rows2,
            rows1,
            rows1,
            rows1,
            rows2,
            rows2,
            rows1,
        ),
        check_vma=False,
    )
```

time: 1040 us -> 562 us (0.54)
  waiting for transfers between devices: 360 us -> 0.01 us
  blocking collectives: 201 us -> 0 us
  Pallas kernels: 208 us -> 391 us
  matrix products: 165 us -> 82.7 us
  between operations: 16.9 us -> 3.2 us
  other arithmetic: 44.8 us -> 33.4 us
    pallas_call x8 -> x11, Pallas kernels: 208 us -> 391 us  [the longest x1 127 us: scatter_grads(): pl.pallas_call(grads_kernel, out_shape=jax.ShapeDtypeStruct((GROUP, 16, w...]
    unnamed x2 -> x0, blocking collectives: 182 us -> none
    reduce_scatter x5 -> x0, waiting for transfers between devices: 177 us -> none  [the longest x4 177 us: scatter_weight(): lax.psum_scatter(a.astype(bf16), PLANE, scatter_dimension=0, tiled=True)]
    all_gather x5 -> x0, waiting for transfers between devices: 174 us -> none  [the longest x4 174 us: gather_weight(): return lax.all_gather(a, PLANE, axis=0, tiled=True)]
    dot_general x6 -> x0, matrix products: 85.8 us -> none  [the longest x1 27.6 us: local(): g_q = jnp.einsum('nts,sd->tnd', g_raw, k_all, preferred_element_type=f32)]
    all_to_all x1 -> x0, blocking collectives: 18.8 us -> none  [swap(): return lax.all_to_all(a, TP, split_axis=0, concat_axis=0, tiled=True)]
    dot_general x4, matrix products: 20.2 us -> 36 us  [dot_nt(): lax.dot_general(a, b, (((1,), (1,)), ((), ())), preferred_element_type=f32)]
  transfers between devices with their start and end apart: 11 -> 2, of which waited for: 6 -> 0; matrix products, arithmetic and copies ran while one was open for 13% -> 4% of each run, Pallas kernels for 15% -> 8%
where the time goes in v2:
time: 562 us; the launch traced here: 552 us
  Pallas kernels  391 us (70%)
  matrix products  82.7 us (15%)
  local copies, waits for them, and re-layouts  37 us (7%)
  other arithmetic  33.4 us (6%)
    pallas_call x1, Pallas kernels, scatter_grads(): pl.pallas_call(grads_kernel, out_shape=jax.ShapeDtypeStruct((GROUP, 16, w...  127 us
    pallas_call x4, Pallas kernels, scatter_rows(): pl.pallas_call(rs_kernel, out_shape=jax.ShapeDtypeStruct((ROWS, n), f32),...  90.2 us
    pallas_call x1, Pallas kernels, front(): pl.pallas_call(front_kernel, out_shape=(jax.ShapeDtypeStruct((GROUP, ROWS...  88.1 us
    pallas_call x3, Pallas kernels, gather_rows(): pl.pallas_call(gather_kernel, out_shape=jax.ShapeDtypeStruct((GROUP, ROWS...  70.3 us
    dot_general x4, matrix products, dot_nt(): lax.dot_general(a, b, (((1,), (1,)), ((), ())), preferred_element_type=f32)  36 us
    dot_general x4, matrix products, dot(): return jnp.dot(a, b, preferred_element_type=f32)  26.5 us
    dot_general x4, matrix products, dot_tn(): lax.dot_general(a, b, (((0,), (0,)), ((), ())), preferred_element_type=f32)  20.2 us
    unnamed x77, local copies, waits for them, and re-layouts  17.8 us
  transfers between devices with their start and end apart: 2, of which 0 were waited for; matrix products, arithmetic and copies ran while one was open for 4% of the time, Pallas kernels for 8%

profile of v2, /device:TPU:1, one launch (start us, length us, event | category | flops | bytes accessed | tf_op | source)
XLA Modules:
  0.0 552.4 jit_solution(13425262328049340448)
XLA Ops:
  0.7 0.9 reduce-window.4
  3.4 1.0 fusion.46
  5.8 0.7 convert_element_type.136
  6.4 1.2 fusion.24
  7.7 1.1 fusion.27
  8.8 2.0 fusion.19.x_ref
  11.0 0.8 bitcast_dynamic-update-slice_fusion.5
  11.9 0.9 copy-done.21
  12.8 88.1 %front.1 = (bf16[8,128,2048]{2,1,0:T(8,128)(2,1)}, bf16[4,4,128,3200]{3,2,1,0:T(8,128)(2,1)}) custom-call(bf16[128,2048]{1,0:T(8,128)(2,1)} %fusion.19.x_ref, bf16[8,16,3200]{2,1,0:T(8,128)(2,1)} %bitcast.166), custom_call_target="tpu_custom_call" | custom-call | tf_op jit(solution)/shard_map/front/pallas_call | solution.py:362
  100.9 1.2 slice.122
  102.1 5.2 fusion.15
  107.5 0.7 compare_select_fusion.1
  109.2 2.4 fusion.38
  111.9 3.9 collective-permute-start
  115.8 1.1 slice.118
  117.0 1.0 copy.96.qseg_ref
  118.7 1.3 copy.98.kseg_ref
  120.0 23.4 %gather_rows.4 = bf16[8,128,2048]{2,1,0:T(8,128)(2,1)} custom-call(bf16[128,2048]{1,0:T(8,128)(2,1)} %x_ref.1), custom_call_target="tpu_custom_call" | custom-call | tf_op jit(solution)/shard_map/gather_rows/pallas_call | solution.py:651
  143.8 1.0 multiply_cosine_fusion.1
  145.6 1.0 copy.112.q_ref
  146.6 5.4 attend.1
  151.9 2.7 convolution_convert_fusion.2
  154.6 22.9 %shard_map.186 = f32[128,2048]{1,0:T(8,128)S(1)} custom-call(bf16[8,128,2048]{2,1,0:T(8,128)(2,1)S(1)} %bitcast.145), custom_call_target="tpu_custom_call" | custom-call | tf_op jit(solution)/shard_map/pallas_call | solution.py:703
  177.7 0.9 multiply_convert_fusion.1.x_ref
  178.7 23.4 %gather_rows.3 = bf16[8,128,2048]{2,1,0:T(8,128)(2,1)} custom-call(bf16[128,2048]{1,0:T(8,128)(2,1)} %multiply_convert_fusion.1.x_ref), custom_call_target="tpu_custom_call" | custom-call | tf_op jit(solution)/shard_map/gather_rows/pallas_call | solution.py:651
  202.1 10.2 %fusion.2 = f32[1024,1536]{1,0:T(8,128)S(1)} fusion(bf16[1024,2048]{1,0:T(8,128)(2,1)} %bitcast.156, bf16[2048,3200]{1,0:T(8,128)(2,1)} %bitcast.178), kind=kOutput, calls=%fused_computation.4 | convolution fusion | flops 6442450944 | bytes 16777216 | tf_op jit(solution)/shard_map/dot_general | solution.py:81
  212.3 6.6 %bitcast_multiply_fusion.1 = (f32[1024,768]{1,0:T(8,128)S(1)}, f32[1024,768]{1,0:T(8,128)S(1)}, bf16[1024,768]{1,0:T(8,128)(2,1)S(1)}) fusion(f32[1024,1536]{1,0:T(8,128)S(1)} %fusion.2, bf16[1024,2048]{1,0:T(8,128)(2,1)S(1)} %bitcast.154, bf16[2048,3200]{1,0:T(8,128)(2,1)} %bitcast.179), kind=kOutput, calls=%fused_computation.15 | convolution fusion | flops 3232235520 | bytes 21495808 | tf_op jit(solution)/shard_map/dot_general | solution.py:81
  218.9 9.1 %convolution_convert_fusion = bf16[2048,1536]{1,0:T(8,128)(2,1)} fusion(bf16[1024,2048]{1,0:T(8,128)(2,1)S(1)} %bitcast.157, f32[1024,768]{1,0:T(8,128)S(1)} %get-tuple-element.28, f32[1024,768]{1,0:T(8,128)S(1)} %get-tuple-element.27), kind=kOutput, calls=%fused_computation | convolution fusion | flops 6448742400 | bytes 16777216 | tf_op jit(solution)/shard_map/dot_general | solution.py:89
  228.1 20.4 %fusion.4 = bf16[1024,2048]{1,0:T(8,128)(2,1)S(1)} fusion(bf16[2048,3200]{1,0:T(8,128)(2,1)} %bitcast.180, f32[1024,768]{1,0:T(8,128)S(1)} %get-tuple-element.28, f32[1024,768]{1,0:T(8,128)S(1)} %get-tuple-element.27), kind=kOutput, calls=%fused_computation.7 | convolution fusion | flops 6447693824 | bytes 16777216 | tf_op jit(solution)/shard_map/dot_general | solution.py:85
  248.5 4.9 fusion.10
  253.4 6.9 %convolution_convert_fusion.3 = bf16[1024,2048]{1,0:T(8,128)(2,1)} fusion(bf16[1024,768]{1,0:T(8,128)(2,1)S(1)} %get-tuple-element.29, bf16[2048,3200]{1,0:T(8,128)(2,1)} %bitcast.181), kind=kOutput, calls=%fused_computation.10 | convolution fusion | flops 3223322624 | bytes 8912896 | tf_op jit(solution)/shard_map/dot_general | solution.py:85
  260.3 22.8 %shard_map.188 = f32[128,2048]{1,0:T(8,128)S(1)} custom-call(bf16[8,128,2048]{2,1,0:T(8,128)(2,1)S(1)} %bitcast.148), custom_call_target="tpu_custom_call" | custom-call | tf_op jit(solution)/shard_map/pallas_call | solution.py:703
  283.4 1.2 fusion.55.x_ref
  284.6 23.4 %gather_rows.5 = bf16[8,128,2048]{2,1,0:T(8,128)(2,1)} custom-call(bf16[128,2048]{1,0:T(8,128)(2,1)} %fusion.55.x_ref), custom_call_target="tpu_custom_call" | custom-call | tf_op jit(solution)/shard_map/gather_rows/pallas_call | solution.py:651
  308.1 4.5 convolution_convert_fusion.7.g_ref
  312.6 10.1 %attend_back.1 = (f32[1024,256]{1,0:T(8,128)}, f32[1024,256]{1,0:T(8,128)}, f32[1024,256]{1,0:T(8,128)}) custom-call(s32[1]{0:T(128)} %bitcast.late_ref, bf16[1024,256]{1,0:T(8,128)(2,1)} %copy.112.q_ref, bf16[1024,256]{1,0:T(8,128)(2,1)} %copy-done.11, bf16[1024,256]{1,0:T(8,128)(2,1)} %collective-permute-done.okv_ref, ...), custom_call_target="tpu_custom_call" | custom-call | tf_op jit(solution)/shard_map/attend_back/pallas_call | solution.py:621
  322.7 2.1 convert_element_type.155
  324.8 1.5 collective-permute-start.1
  326.3 2.5 copy.114
  328.8 1.6 multiply_add_fusion.2
  330.4 1.6 multiply_reduce_fusion
  332.3 4.7 copy.103
  336.9 1.3 copy.113
  338.3 2.2 copy-done
  340.4 22.8 %shard_map.187 = f32[128,2048]{1,0:T(8,128)S(1)} custom-call(bf16[8,128,2048]{2,1,0:T(8,128)(2,1)S(1)} %bitcast.146), custom_call_target="tpu_custom_call" | custom-call | tf_op jit(solution)/shard_map/pallas_call | solution.py:703
  363.3 2.3 convolution_convert_fusion.6
  365.6 1.2 convert_add_fusion.1
  366.9 2.2 fusion.41
  370.1 3.9 convolution_convert_fusion.5
  374.0 6.0 %convolution_convert_fusion.1 = bf16[1024,2048]{1,0:T(8,128)(2,1)} fusion(bf16[2048,3200]{1,0:T(8,128)(2,1)} %bitcast.183, f32[1024,256]{1,0:T(8,128)S(1)} %copy-done.20, f32[1024,128]{1,0:T(8,128)S(1)} %fusion.43, f32[1024,128]{1,0:T(8,128)S(1)} %get-tuple-element.43), kind=kOutput, calls=%fused_computation.8 | convolution fusion | flops 2151153664 | bytes 8388608 | tf_op jit(solution)/shard_map/dot_general | solution.py:85
  380.1 3.3 constant_dynamic-update-slice_fusion.7
  383.6 0.9 constant_dynamic-update-slice_fusion.6
  384.5 1.1 constant_dynamic-update-slice_fusion.5
  385.6 6.2 %constant_dynamic-update-slice_fusion.4 = bf16[4,4,128,3200]{3,2,1,0:T(8,128)(2,1)} fusion(bf16[4,4,128,3200]{3,2,1,0:T(8,128)(2,1)} %constant_dynamic-update-slice_fusion.5, bf16[4,4,128,1536]{3,2,1,0:T(8,128)(2,1)} %bitcast.151), kind=kLoop, calls=%fused_computation.118 | loop fusion | bytes 12582912
  391.8 2.0 constant_dynamic-update-slice_fusion.3.p_ref
  393.7 126.7 %grads.1 = bf16[8,16,3200]{2,1,0:T(8,128)(2,1)} custom-call(bf16[4,4,128,3200]{3,2,1,0:T(8,128)(2,1)} %constant_dynamic-update-slice_fusion.3.p_ref), custom_call_target="tpu_custom_call" | custom-call | tf_op jit(solution)/shard_map/grads/pallas_call | solution.py:468
  520.5 1.4 convert_element_type.164
  522.1 0.8 copy-done.1
  522.9 21.7 %shard_map.189 = f32[128,2048]{1,0:T(8,128)S(1)} custom-call(bf16[8,128,2048]{2,1,0:T(8,128)(2,1)S(1)} %bitcast.147), custom_call_target="tpu_custom_call" | custom-call | tf_op jit(solution)/shard_map/pallas_call | solution.py:703
  545.5 0.8 copy.133
  546.3 0.7 copy.130
  547.0 1.4 fusion.47
  548.6 1.6 fusion.28
  550.2 1.8 fusion.23
  (122 shorter events, 8.6 us)
Async XLA Ops:
  0.6 11.2 %copy-start.23 = (bf16[16,6144]{1,0:T(8,128)(2,1)S(1)}, bf16[16,6144]{1,0:T(8,128)(2,1)}, u32[]{:S(2)}) copy-start(bf16[16,6144]{1,0:T(8,128)(2,1)} %param.20) | copy-start | bytes 589828
  11.9 0.9 copy-start.21
  102.1 5.4 copy-start.25
  107.3 36.3 %copy-start.4 = (f32[1024,512]{0,1:T(8,128)}, f32[1024,512]{0,1:T(8,128)S(1)}, u32[]{:S(2)}) copy-start(f32[1024,512]{0,1:T(8,128)S(1)} %fusion.15) | copy-start | bytes 6291460
  108.7 9.4 %copy-start.6 = (f32[1024,128]{1,0:T(8,128)}, f32[1024,128]{1,0:T(8,128)S(1)}, u32[]{:S(2)}) copy-start(f32[1024,128]{1,0:T(8,128)S(1)} %copy.118) | copy-start | bytes 1572868
  109.2 34.3 %copy-start.24 = (s32[1024]{0:T(1024)}, s32[1024]{0:T(1024)S(1)}, u32[]{:S(2)}) copy-start(s32[1024]{0:T(1024)S(1)} %get-tuple-element.60) | copy-start | bytes 12292
  111.9 31.6 %copy-start.11 = (bf16[1024,256]{1,0:T(8,128)(2,1)}, bf16[1024,256]{1,0:T(8,128)(2,1)S(1)}, u32[]{:S(2)}) copy-start(bf16[1024,256]{1,0:T(8,128)(2,1)S(1)} %pad_maximum_fusion.1.kv_ref) | copy-start | bytes 1572868
  111.9 34.7 %collective-permute-start = (bf16[1024,256]{1,0:T(8,128)(2,1)S(1)}, bf16[1024,256]{1,0:T(8,128)(2,1)}, u32[]{:S(2)}, u32[]{:S(2)}) collective-permute-start(bf16[1024,256]{1,0:T(8,128)(2,1)S(1)} %pad_maximum_fusion.1.kv_ref), channel_id=1, source_target_pairs={{0,8},{1,9},{2,10},{3,11},{4,12},{5,13},{6,14},{7,15},{16,24},{17,... | collective-permute-start | bytes 1572872 | tf_op jit(solution)/shard_map/ppermute | solution.py:798
  144.8 0.7 copy-start.16
  154.6 22.9 %copy-start.2 = (bf16[128,2048]{1,0:T(8,128)(2,1)S(1)}, bf16[128,2048]{1,0:T(8,128)(2,1)}, u32[]{:S(2)}) copy-start(bf16[128,2048]{1,0:T(8,128)(2,1)} %param.11) | copy-start | bytes 1572868
  202.1 10.2 %copy-start.13 = (bf16[8,128,2048]{2,1,0:T(8,128)(2,1)S(1)}, bf16[8,128,2048]{2,1,0:T(8,128)(2,1)}, u32[]{:S(2)}) copy-start(bf16[8,128,2048]{2,1,0:T(8,128)(2,1)} %gather_rows.4) | copy-start | bytes 12582916
  212.3 6.6 %copy-start.14 = (bf16[8,128,2048]{2,1,0:T(8,128)(2,1)S(1)}, bf16[8,128,2048]{2,1,0:T(8,128)(2,1)}, u32[]{:S(2)}) copy-start(bf16[8,128,2048]{2,1,0:T(8,128)(2,1)} %gather_rows.3) | copy-start | bytes 12582916
  260.3 23.1 %copy-start.9 = (bf16[128,2048]{1,0:T(8,128)(2,1)S(1)}, bf16[128,2048]{1,0:T(8,128)(2,1)}, u32[]{:S(2)}) copy-start(bf16[128,2048]{1,0:T(8,128)(2,1)} %x_ref.1) | copy-start | bytes 1572868
  312.6 17.7 %slice-start = ((f32[1024,512]{0,1:T(8,128)}), f32[1024,256]{0,1:T(8,128)S(1)}, s32[]{:S(2)}) async-start(f32[1024,512]{0,1:T(8,128)} %copy-done.4), calls=%async_computation | async-start | bytes 2097152 | tf_op jit(solution)/shard_map/jvp()/slice | solution.py:68
  324.8 40.8 %collective-permute-start.1 = (bf16[1024,256]{1,0:T(8,128)(2,1)}, bf16[1024,256]{1,0:T(8,128)(2,1)}, u32[]{:S(2)}, u32[]{:S(2)}) collective-permute-start(bf16[1024,256]{1,0:T(8,128)(2,1)} %convert_element_type.155), channel_id=1, source_target_pairs={{8,0},{9,1},{10,2},{11,3},{12,4},{13,5},{14,6},{15,7},{24,16},{25,... | collective-permute-start | bytes 1572872 | tf_op jit(solution)/shard_map/ppermute | solution.py:821
  328.8 3.2 copy-start.5
  338.3 2.2 copy-start
  340.4 22.8 %copy-start.12 = (bf16[8,128,2048]{2,1,0:T(8,128)(2,1)S(1)}, bf16[8,128,2048]{2,1,0:T(8,128)(2,1)}, u32[]{:S(2)}) copy-start(bf16[8,128,2048]{2,1,0:T(8,128)(2,1)} %gather_rows.5) | copy-start | bytes 12582916
  340.4 22.8 %copy-start.15 = (bf16[1024,256]{1,0:T(8,128)(2,1)S(1)}, bf16[1024,256]{1,0:T(8,128)(2,1)}, u32[]{:S(2)}) copy-start(bf16[1024,256]{1,0:T(8,128)(2,1)} %attend.1) | copy-start | bytes 1572868
  363.3 2.3 copy-start.19
  365.6 3.5 copy-start.7
  366.8 3.3 copy-start.20
  366.8 3.3 copy-start.26
  380.1 4.4 copy-start.18
  385.6 6.2 %copy-start.8 = (bf16[2048,768]{1,0:T(8,128)(2,1)S(1)}, bf16[2048,768]{1,0:T(8,128)(2,1)}, u32[]{:S(2)}) copy-start(bf16[2048,768]{1,0:T(8,128)(2,1)} %copy.103) | copy-start | bytes 9437188
  520.5 2.4 copy-start.1
  521.9 22.7 %copy-start.3 = (bf16[128,2048]{1,0:T(8,128)(2,1)S(1)}, bf16[128,2048]{1,0:T(8,128)(2,1)}, u32[]{:S(2)}) copy-start(bf16[128,2048]{1,0:T(8,128)(2,1)} %param.11) | copy-start | bytes 1572868
  522.9 24.1 %copy-start.22 = (bf16[16,4096]{1,0:T(8,128)(2,1)S(1)}, bf16[16,4096]{1,0:T(8,128)(2,1)}, u32[]{:S(2)}) copy-start(bf16[16,4096]{1,0:T(8,128)(2,1)} %param.14) | copy-start | bytes 393220
  544.6 4.0 copy-start.17
  544.9 5.3 copy-start.10
